TPU v7x, 256 devices: a whole 4x4x8 slice. The times are simulated.
256 devices in a mesh: node: 32 (over z, x), local: 8 (over y, core).
Axes of the slice: x: 4, y: 4, z: 8, core: 2. Of those that a mesh axis runs over, the one named last changes fastest.
Arguments:
- pooled_grad: bfloat16 [131072, 128], P(('node', 'local')), may hold values from -40 to 40, as said below
- lengths: int32 [131072], P(('node', 'local')), may hold values from 1 to 32
- slot_of: int32 [131072, 32], P(('node', 'local')), may hold values from 0 to 16383, as said below
- slot_row: int32 [524288], P(('node', 'local')), may hold values from 0 to 1048575, as said below
- table: float32 [1048576, 128], P(('node', 'local')), may hold values from -6 to 6
- accum: float32 [1048576], P(('node', 'local')), may hold values from 0.05 to 2
Outputs:
- table_new: float32 [1048576, 128], P(('node', 'local'))
- accum_new: float32 [1048576], P(('node', 'local'))
Inputs may be any that keep to these rules, and one draw needn't show every extreme that they name: `pooled_grad`: spread over rows and columns. `slot_row`: slot u of node m's table, u = l * 2048 + n * 64 + c with c < 64, holds a row of device n * 8 + l (rows d * 4096 to (d + 1) * 4096 - 1 belong to device d); this group of 64 slots is the bucket (m, l, n). Ids name only the first live slots of each bucket; bucket (m, l, (m + 1) % 32) has all 64 live, every other bucket one to 32 live, and bucket (m, l, (m + 2) % 32) exactly 32. An id position of a sample of node m names slot slot_of of node m's table.
All inputs are finite; a program needn't handle non-finite values.
Results may differ from a plain program's by a relative error of at most 0.0003.
Values may be sent and summed in bfloat16 or wider, within the bound.
No kernel may reach another device: no remote copies, remote signals or barrier semaphores. Data moves between devices by JAX's collectives and lax.ppermute only.
A program may use at most 64 MiB of HBM per device.

v0:
```python
import jax
import jax.numpy as jnp
from jax import lax
from jax.sharding import PartitionSpec as P

LEARN_RATE = 0.3
EPSILON = 1e-06


def slot_counts(slot_ids, bag_lens, lowest, how_many):
    positions = jnp.arange(slot_ids.shape[1], dtype=jnp.int32)
    present = positions[None, :] < bag_lens[:, None]
    offset = slot_ids - lowest
    columns = jnp.arange(how_many, dtype=jnp.int32)
    matched = (offset[:, :, None] == columns[None, None, :]) & present[:, :, None]
    return jnp.sum(matched.astype(jnp.float32), axis=1).astype(jnp.bfloat16)


def weighted_sums(counts, pooled):
    return lax.dot_general(
        counts, pooled, (((0,), (0,)), ((), ())), preferred_element_type=jnp.float32
    )


def per_device(pooled_grad, lengths, slot_of, slot_row, table, accum):
    slots_agg = slot_row.shape[0]
    lowest = lax.axis_index("local") * slots_agg
    pooled = lax.all_gather(pooled_grad, "local", axis=0, tiled=True)
    slot_ids = lax.all_gather(slot_of, "local", axis=0, tiled=True)
    bag_lens = lax.all_gather(lengths, "local", axis=0, tiled=True)
    summed = weighted_sums(slot_counts(slot_ids, bag_lens, lowest, slots_agg), pooled)
    got_grads, got_rows = (
        lax.all_to_all(summed, "node", split_axis=0, concat_axis=0, tiled=True),
        lax.all_to_all(slot_row, "node", split_axis=0, concat_axis=0, tiled=True),
    )
    local_rows = got_rows % table.shape[0]
    gradient = jnp.zeros(table.shape, jnp.float32).at[local_rows].add(got_grads)
    accum_new = accum + jnp.mean(gradient * gradient, axis=1)
    table_new = table - LEARN_RATE * gradient / (jnp.sqrt(accum_new)[:, None] + EPSILON)
    return (table_new, accum_new)


def solution(mesh):
    return jax.shard_map(
        per_device,
        mesh=mesh,
        in_specs=(
            P(("node", "local"), None),
            P(("node", "local")),
            P(("node", "local"), None),
            P(("node", "local")),
            P(("node", "local"), None),
            P(("node", "local")),
        ),
        out_specs=(P(("node", "local"), None), P(("node", "local"))),
        check_vma=False,
    )
```

profile of v0, /device:TPU:24, one launch (start us, length us, event | category | flops | bytes accessed | tf_op | source)
XLA Modules:
  0.0 404.5 jit_solution(13359477460584208686)
XLA Ops:
  7.2 0.0 all-gather.3.cloned.1.call-start
  7.2 0.7 all-gather.3.cloned.1.call-update
  7.9 1.4 all_to_all.16
  9.3 11.3 %all-to-all-start = ((s32[32,64,1]{1,2,0:T(1,128)}), s32[32,64,1]{1,2,0:T(1,128)S(1)}, u32[]{:S(2)}, u32[]{:S(2)}) async-start(s32[32,64,1]{1,2,0:T(1,128)} %bitcast), calls=%async_computation | async-start | bytes 32768 | tf_op jit(solution)/shard_map/all_to_all | solution.py:34
  20.6 0.0 copy-start.2
  20.6 13.9 %all_gather.9 = s32[4096,32]{0,1:T(8,128)S(1)} all-gather(s32[512,32]{0,1:T(8,128)} %param.8), channel_id=1, replica_groups=mesh['node'=32,'local'=8] {'local'}, dimensions={0}, use_global_device_ids=true | all-gather | bytes 589824 | tf_op jit(solution)/shard_map/all_gather | solution.py:29
  34.6 0.6 copy.13
  35.2 0.0 copy-done.2
  35.2 11.0 %all-gather = s32[8,1,512]{2,1,0:T(1,128)S(1)} all-gather(s32[1,1,512]{2,1,0:T(1,128)S(1)} %bitcast.12), channel_id=1, replica_groups=mesh['node'=32,'local'=8] {'local'}, dimensions={0}, use_global_device_ids=true | all-gather | bytes 18432 | tf_op jit(solution)/shard_map/all_gather | solution.py:30
  46.2 0.1 iota_compare_fusion.1
  46.2 0.8 copy.14
  47.1 284.9 %convert_reduce_fusion = bf16[4096,2048]{1,0:T(8,128)(2,1)} fusion(s32[4096,32]{1,0:T(8,128)S(1)} %copy.13, pred[4096,32]{1,0:T(8,128)(4,1)S(1)} %copy.14), kind=kLoop, calls=%fused_computation.1 | loop fusion | flops 1065353216 | bytes 17432576 | tf_op jit(solution)/shard_map/reduce_sum | solution.py:16
  332.0 0.0 all-gather.3.cloned.1.call-done
  332.0 11.6 %fusion.6 = f32[2048,128]{1,0:T(8,128)} fusion(bf16[4096,2048]{1,0:T(8,128)(2,1)} %convert_reduce_fusion, bf16[4096,128]{1,0:T(8,128)(2,1)} %all-gather.3.cloned.1.call-done), kind=kOutput, calls=%fused_computation.19 | convolution fusion | flops 2147483648 | bytes 18874368 | tf_op jit(solution)/shard_map/dot_general | solution.py:20
  343.6 0.0 all-to-all-done
  343.6 10.5 %all-to-all-start.1 = ((f32[32,64,128]{2,1,0:T(8,128)}), f32[32,64,128]{2,1,0:T(8,128)S(1)}, u32[]{:S(2)}, u32[]{:S(2)}) async-start(f32[32,64,128]{2,1,0:T(8,128)} %bitcast.4), calls=%async_computation.1 | async-start | bytes 2097152 | tf_op jit(solution)/shard_map/all_to_all | solution.py:33
  354.1 0.5 broadcast.77
  354.6 0.7 reduce.3
  355.3 0.1 all_to_all.18
  355.4 27.0 %all-to-all-done.1 = f32[32,64,128]{2,1,0:T(8,128)S(1)} async-done(((f32[32,64,128]{2,1,0:T(8,128)}), f32[32,64,128]{2,1,0:T(8,128)S(1)}, u32[]{:S(2)}, u32[]{:S(2)}) %all-to-all-start.1) | async-done | bytes 1048608 | tf_op jit(solution)/shard_map/all_to_all | solution.py:33
  382.4 0.0 copy-start.1
  382.4 12.0 %scatter_custom_fusion = f32[4096,128]{1,0:T(8,128)S(1)} fusion(s32[2048]{0:T(1024)S(1)} %bitcast.11, f32[2048,128]{1,0:T(8,128)S(1)} %bitcast.9, f32[]{:T(128)} %constant.10.clone.1), kind=kCustom, calls=%fused_computation.8 | custom fusion | flops 262144 | bytes 2097156 | tf_op jit(solution)/shard_map/scatter-add | solution.py:37
  394.4 0.0 copy-start
  394.4 0.6 multiply_reduce_fusion
  395.0 0.0 copy-done.1
  395.0 0.6 sqrt_add_fusion
  395.6 0.3 copy-done
  396.0 1.7 divide_subtract_fusion
  (2 shorter events, 0.1 us)
Async XLA Ops:
  7.2 324.8 %all-gather.3.cloned.1.call-start = ((), (), s32[]{:S(2)}) async-start(), calls=%async_computation.2 | async-start | bytes 1179648 | tf_op jit(solution)/shard_map/all_gather | solution.py:28
  9.3 334.3 %all-to-all-start = ((s32[32,64,1]{1,2,0:T(1,128)}), s32[32,64,1]{1,2,0:T(1,128)S(1)}, u32[]{:S(2)}, u32[]{:S(2)}) async-start(s32[32,64,1]{1,2,0:T(1,128)} %bitcast), calls=%async_computation | async-start | bytes 32768 | tf_op jit(solution)/shard_map/all_to_all | solution.py:34
  20.6 14.6 %copy-start.2 = (s32[512]{0:T(512)S(1)}, s32[512]{0:T(512)}, u32[]{:S(2)}) copy-start(s32[512]{0:T(512)} %param.7) | copy-start | bytes 6148
  343.6 38.8 %all-to-all-start.1 = ((f32[32,64,128]{2,1,0:T(8,128)}), f32[32,64,128]{2,1,0:T(8,128)S(1)}, u32[]{:S(2)}, u32[]{:S(2)}) async-start(f32[32,64,128]{2,1,0:T(8,128)} %bitcast.4), calls=%async_computation.1 | async-start | bytes 2097152 | tf_op jit(solution)/shard_map/all_to_all | solution.py:33
  382.4 12.6 %copy-start.1 = (f32[4096]{0:T(1024)S(1)}, f32[4096]{0:T(1024)}, u32[]{:S(2)}) copy-start(f32[4096]{0:T(1024)} %param.11) | copy-start | bytes 49156
  394.4 1.6 copy-start
Sparse Core Ops, SparseCore 0:
  9.9 27.4 all-gather.2
where the time goes:
time: 406 us; the launch traced here: 404 us
  other arithmetic  301 us (74%)
  waiting for transfers between devices  27.7 us (7%)
  blocking collectives  24.9 us (6%)
  starting transfers between devices  21.8 us (5%)
  between operations  14.1 us (3%)
  matrix products  11.6 us (3%)
    reduce_sum x1, other arithmetic, slot_counts(): return jnp.sum(matched.astype(jnp.float32), axis=1).astype(jnp.bfloat16)  285 us
    all_to_all x1, waiting for transfers between devices, per_device(): lax.all_to_all(summed, 'node', split_axis=0, concat_axis=0, tiled=True)  27 us
    all_gather x1, blocking collectives, per_device(): slot_ids = lax.all_gather(slot_of, 'local', axis=0, tiled=True)  13.9 us
    scatter-add x1, other arithmetic, per_device(): gradient = jnp.zeros(table.shape, jnp.float32).at[local_rows].add(got_grads)  12 us
    dot_general x1, matrix products, weighted_sums(): lax.dot_general(counts, pooled, (((0,), (0,)), ((), ())), preferred_eleme...  11.6 us
    all_to_all x1, starting transfers between devices, per_device(): lax.all_to_all(slot_row, 'node', split_axis=0, concat_axis=0, tiled=True)  11.3 us
    all_gather x1, blocking collectives, per_device(): bag_lens = lax.all_gather(lengths, 'local', axis=0, tiled=True)  11 us
    all_to_all x1, starting transfers between devices, per_device(): lax.all_to_all(summed, 'node', split_axis=0, concat_axis=0, tiled=True)  10.5 us
  transfers between devices with their start and end apart: 3, of which 1 were waited for; matrix products, arithmetic and copies ran while one was open for 74% of the time, Pallas kernels for 0%

commit v1 on v0

v1 whole, which is shorter than its diff:
```python
import jax
import jax.numpy as jnp
from jax import lax
from jax.experimental import pallas as pl
from jax.experimental.pallas import tpu as pltpu
from jax.sharding import PartitionSpec as P

LEARN_RATE = 0.3
EPSILON = 1e-06

LANES = 128
KEEP = 32
GROUP = 8
BLOCKS = 17
OWN = 9 * LANES
BUCKET_ROWS = 40
F32, BF16, I32 = jnp.float32, jnp.bfloat16, jnp.int32


def rows_iota(rows, cols):
    return lax.broadcasted_iota(I32, (rows, cols), 0)


def lanes_iota(rows, cols):
    return lax.broadcasted_iota(I32, (rows, cols), 1)


def prep_kernel(slot_ref, len_ref, pooled_ref, out_ref, perm_ref):
    slot = slot_ref[...]
    present = rows_iota(*slot.shape) < len_ref[...]
    side = (slot >> 11) & 1
    owner = (slot >> 6) & 31
    place = slot & 63
    first = place < KEEP
    low = jnp.where(first, (owner & 3) * KEEP + place, side * KEEP + place - KEEP)
    low = jnp.where(present, low, -1)
    block = (slot >> 12) * BLOCKS + jnp.where(first, side * 8 + (owner >> 2), 16)

    def by_group(x):
        parts = [x[:, LANES * b : LANES * (b + 1)] for b in range(4)]
        return jnp.concatenate(parts, axis=0).T.astype(BF16)

    out_ref[512:640, :] = by_group(low.astype(F32))
    out_ref[640:768, :] = by_group(block.astype(F32))
    for h in range(2):
        for b in range(4):
            start = b * 128 + h * 64
            perm_ref[pl.ds(h * 4 + b, 64, stride=GROUP), :] = pooled_ref[start : start + 64, :].astype(F32)
    for t in range(4):
        out_ref[t * 128 : (t + 1) * 128, :] = perm_ref[t * 128 : (t + 1) * 128, :].T.astype(BF16)


def sums_kernel(place_ref, got_ref, own_ref, other_ref, low_ref, code_ref, counts_ref):
    chip, core = place_ref[0], place_ref[1]
    for ch in range(4):
        base = ch * 768
        low_ref[ch * 128 : (ch + 1) * 128, :] = got_ref[base + 512 : base + 640, :].astype(F32)
        block = got_ref[base + 640 : base + 768, :].astype(F32).astype(I32) - chip * BLOCKS
        valid = (block >= 0) & (block < BLOCKS)
        block = jnp.where(block < 16, block ^ (core * 8), block)
        member = (rows_iota(128, 128) >> 6) * 4 + (lanes_iota(128, 128) >> 5)
        code = jnp.where(valid, block * GROUP + member, -1)
        code_ref[ch * 128 : (ch + 1) * 128, :] = code.astype(F32)

    tiles = [(rows_iota(16, 128) + 16 * t).astype(F32).astype(BF16) for t in range(9)]
    one, zero = jnp.ones((16, 128), BF16), jnp.zeros((16, 128), BF16)

    def onehot(ref, row, count):
        halves = []
        for h in range(2):
            line = ref[pl.ds(row + h * 64, 1), :]
            line = jnp.broadcast_to(line, (16, 128)).astype(BF16)
            halves.append(jnp.concatenate([jnp.where(line == tiles[t], one, zero) for t in range(count)], axis=0))
        return jnp.concatenate(halves, axis=1)

    def group_counts(row):
        return lax.dot_general(
            onehot(code_ref, row, 9), onehot(low_ref, row, 8), (((1,), (1,)), ((), ())), preferred_element_type=F32
        )

    def step(i, carry):
        ch, pair = i // 32, i % 32
        row = ch * 128 + pair * 2
        first, second = group_counts(row), group_counts(row + 1)
        at = pl.multiple_of(i * 16, 16)
        for b in range(BLOCKS):
            both = jnp.concatenate([first[b * 8 : b * 8 + 8, :], second[b * 8 : b * 8 + 8, :]], axis=0)
            counts_ref[pl.ds(at, 16), b * 128 : (b + 1) * 128] = both.astype(BF16)
        return carry

    lax.fori_loop(0, 128, step, 0, unroll=4)

    pooled = jnp.concatenate(
        [got_ref[ch * 768 + t * 128 : ch * 768 + (t + 1) * 128, :] for ch in range(4) for t in range(4)], axis=1
    )
    total = jnp.dot(pooled, counts_ref[...], preferred_element_type=F32)
    own_ref[:, :1024] = total[:, :1024]
    other_ref[:, :1024] = total[:, 1024:2048]
    own_ref[:, 1024:] = total[:, 2048:]
    other_ref[:, 1024:] = total[:, 2048:]


def code_kernel(place_ref, own_ref, got_ref, row_ref, out_ref, over_ref):
    core, node = place_ref[1], place_ref[2]
    rows = row_ref[...] & 4095
    next_node = (node + 1) & 31

    def coded(b):
        total = own_ref[:, b * 128 : (b + 1) * 128] + got_ref[:, b * 128 : (b + 1) * 128]
        most = jnp.max(jnp.abs(total), axis=0, keepdims=True)
        power = jnp.floor(jnp.log2(jnp.maximum(most, 1e-30))) + 1.0
        scaled = jnp.clip(jnp.round(total * jnp.exp2(15.0 - power)), -32767.0, 32767.0)
        return scaled.T.astype(I32).astype(jnp.int16), power.astype(I32)

    def tail(row_line, power_line):
        at = rows_iota(8, 128)
        out = jnp.where(at == 0, jnp.broadcast_to(row_line, (8, 128)), jnp.broadcast_to(power_line, (8, 128)))
        return out

    for b in range(8):
        codes, power = coded(b)
        for q in range(4):
            n = b * 4 + q
            out_ref[n, 0:32, :] = codes[q * 32 : (q + 1) * 32, :]
            out_ref[n, 32:40, :] = tail(rows[n >> 1 : (n >> 1) + 1, :], power).astype(jnp.int16)
    codes, power = coded(8)
    over_ref[0:64, :] = codes[0:64, :]
    over_ref[64:72, :] = tail(row_ref[pl.ds(next_node >> 1, 1), :] & 4095, power).astype(jnp.int16)


def update_kernel(place_ref, got_ref, over_ref, table_ref, accum_ref, table_out, accum_out, value_ref, line_ref):
    core, node = place_ref[1], place_ref[2]
    rb = pl.program_id(0)

    @pl.when(rb == 0)
    def _():
        def halves(x):
            x = x.astype(I32)
            return (x >> 8).astype(F32).astype(BF16), (x & 255).astype(F32).astype(BF16)

        for m in range(32):
            high, low = halves(got_ref[m, 0:32, :])
            value_ref[m * 32 : (m + 1) * 32, 0:128] = high
            value_ref[m * 32 : (m + 1) * 32, 128:256] = low
        start = pl.multiple_of(core * 32, 32)
        high, low = halves(over_ref[pl.ds(start, 32), :])
        value_ref[1024:1056, 0:128] = high
        value_ref[1024:1056, 128:256] = low
        value_ref[1056:1152, :] = jnp.zeros((96, 256), BF16)

        quarter = lanes_iota(8, 128) >> 5
        ids, powers = jnp.zeros((8, 128), I32), jnp.zeros((8, 128), I32)
        for r in range(4):
            tails = [got_ref[kb * 4 + r, 32:40, :].astype(I32) for kb in range(8)]
            id_lines = jnp.concatenate([t[0:1, :] for t in tails], axis=0)
            power_lines = jnp.concatenate([t[1:2, :] for t in tails], axis=0)
            id_lines = pltpu.roll(id_lines, (r * 32 + 128 - (node & 1) * 64) & 127, axis=1)
            power_lines = pltpu.roll(power_lines, (r * 32 + 128 - (node & 3) * 32) & 127, axis=1)
            ids = jnp.where(quarter == r, id_lines, ids)
            powers = jnp.where(quarter == r, power_lines, powers)
        line_ref[0:8, :] = ids
        line_ref[8:16, :] = powers
        over_tail = over_ref[64:72, :].astype(I32)
        over_ids = pltpu.roll(over_tail, (128 - ((node & 1) * 64 + 32)) & 127, axis=1)
        over_powers = pltpu.roll(over_tail, (128 - core * 32) & 127, axis=1)
        lane = lanes_iota(1, 128)
        line_ref[16:17, :] = jnp.where(lane < 32, over_ids[0:1, :], -1)
        line_ref[17:18, :] = over_powers[1:2, :]

    tiles = [(rows_iota(16, 128) + 16 * t).astype(F32).astype(BF16) for t in range(16)]
    zero = jnp.zeros((16, 128), BF16)
    parts = []
    for kb in range(9):
        at_id, at_power = (kb, kb + 8) if kb < 8 else (16, 17)
        ids = (line_ref[at_id : at_id + 1, :] - rb * 256).astype(F32)
        ids = jnp.broadcast_to(ids, (16, 128)).astype(BF16)
        scale = jnp.exp2(line_ref[at_power : at_power + 1, :].astype(F32) - 15.0)
        scale = jnp.broadcast_to(scale, (16, 128)).astype(BF16)
        parts.append(jnp.concatenate([jnp.where(ids == tiles[t], scale, zero) for t in range(16)], axis=0))
    hot = jnp.concatenate(parts, axis=1)
    both = jnp.dot(hot, value_ref[...], preferred_element_type=F32)
    gradient = both[:, 0:128] * 256.0 + both[:, 128:256]
    for t in range(2):
        g = gradient[t * 128 : (t + 1) * 128, :]
        diag = rows_iota(128, 128) == lanes_iota(128, 128)
        accum = jnp.broadcast_to(accum_ref[pl.ds(rb * 2 + t, 1), :], (128, 128))
        fresh = jnp.sum(g * g * (1.0 / 128.0) + jnp.where(diag, accum, 0.0), axis=1, keepdims=True)
        accum_out[pl.ds(rb * 2 + t, 1), :] = jnp.sum(jnp.where(diag, fresh, 0.0), axis=0, keepdims=True)
        step = LEARN_RATE * g / (jnp.sqrt(fresh) + EPSILON)
        table_out[t * 128 : (t + 1) * 128, :] = table_ref[t * 128 : (t + 1) * 128, :] - step


VMEM = pl.BlockSpec(memory_space=pltpu.VMEM)
SMEM = pl.BlockSpec(memory_space=pltpu.SMEM)
PARAMS = pltpu.CompilerParams(vmem_limit_bytes=40 * 1024 * 1024)


def prep(slot_t, lengths, pooled):
    return pl.pallas_call(
        prep_kernel,
        out_shape=jax.ShapeDtypeStruct((768, 128), BF16),
        in_specs=[VMEM] * 3,
        out_specs=VMEM,
        scratch_shapes=[pltpu.VMEM((512, 128), F32)],
        compiler_params=PARAMS,
        name="prep",
    )(slot_t, lengths, pooled)


def sums(place, got):
    return pl.pallas_call(
        sums_kernel,
        out_shape=[jax.ShapeDtypeStruct((128, OWN), F32)] * 2,
        in_specs=[SMEM, VMEM],
        out_specs=[VMEM] * 2,
        scratch_shapes=[
            pltpu.VMEM((512, 128), F32),
            pltpu.VMEM((512, 128), F32),
            pltpu.VMEM((2048, BLOCKS * 128), BF16),
        ],
        compiler_params=PARAMS,
        name="sums",
    )(place, got)


def code(place, own, got, slot_row):
    return pl.pallas_call(
        code_kernel,
        out_shape=[
            jax.ShapeDtypeStruct((32, BUCKET_ROWS, 128), jnp.int16),
            jax.ShapeDtypeStruct((80, 128), jnp.int16),
        ],
        in_specs=[SMEM] + [VMEM] * 3,
        out_specs=[VMEM] * 2,
        compiler_params=PARAMS,
        name="code",
    )(place, own, got, slot_row)


def update(place, got, over, table, accum):
    whole = lambda shape: pl.BlockSpec(shape, lambda i: (0,) * len(shape))
    return pl.pallas_call(
        update_kernel,
        grid=(16,),
        out_shape=[jax.ShapeDtypeStruct((4096, 128), F32), jax.ShapeDtypeStruct((32, 128), F32)],
        in_specs=[
            SMEM,
            whole((32, BUCKET_ROWS, 128)),
            whole((80, 128)),
            pl.BlockSpec((256, 128), lambda i: (i, 0)),
            whole((32, 128)),
        ],
        out_specs=[pl.BlockSpec((256, 128), lambda i: (i, 0)), whole((32, 128))],
        scratch_shapes=[pltpu.VMEM((1152, 256), BF16), pltpu.VMEM((24, 128), I32)],
        compiler_params=PARAMS,
        name="update",
    )(place, got, over, table, accum)


def per_device(pooled_grad, lengths, slot_of, slot_row, table, accum):
    local, node = lax.axis_index("local"), lax.axis_index("node")
    place = jnp.stack([local >> 1, local & 1, node]).astype(I32)
    packed = prep(slot_of.T, lengths.reshape(1, 512), pooled_grad)
    same_core = [[0, 2, 4, 6], [1, 3, 5, 7]]
    got = lax.all_gather(packed, "local", axis=0, tiled=True, axis_index_groups=same_core)
    own, other = sums(place, got)
    other = lax.ppermute(other, "local", [(i, i ^ 1) for i in range(8)])
    codes, over = code(place, own, other, slot_row.reshape(16, 128))
    over = lax.ppermute(over, "node", [(i, (i + 1) % 32) for i in range(32)])
    codes = lax.all_to_all(codes, "node", split_axis=0, concat_axis=0, tiled=True)
    table_new, accum_new = update(place, codes, over, table, accum.reshape(32, 128))
    return table_new, accum_new.reshape(4096)


def solution(mesh):
    return jax.shard_map(
        per_device,
        mesh=mesh,
        in_specs=(
            P(("node", "local"), None),
            P(("node", "local")),
            P(("node", "local"), None),
            P(("node", "local")),
            P(("node", "local"), None),
            P(("node", "local")),
        ),
        out_specs=(P(("node", "local"), None), P(("node", "local"))),
        check_vma=False,
    )
```

time: 406 us -> 70.2 us (0.17)
  other arithmetic: 301 us -> 0.08 us
  Pallas kernels: 0 us -> 24 us
  between operations: 14.1 us -> 0.69 us
  waiting for transfers between devices: 27.7 us -> 14.7 us
  matrix products: 11.6 us -> 0 us
  blocking collectives: 24.9 us -> 14.2 us
  starting transfers between devices: 21.8 us -> 13.3 us
    reduce_sum x2 -> x0, other arithmetic: 286 us -> none  [the longest x1 285 us: slot_counts(): return jnp.sum(matched.astype(jnp.float32), axis=1).astype(jnp.bfloat16)]
    all_to_all x2 -> x1, waiting for transfers between devices: 27 us -> 2.75 us  [per_device(): lax.all_to_all(codes, 'node', split_axis=0, concat_axis=0, tiled=True)]
    pallas_call x0 -> x4, Pallas kernels: none -> 24 us  [the longest x1 12.3 us: sums(): pl.pallas_call(sums_kernel, out_shape=[jax.ShapeDtypeStruct((128, OWN), F...]
    ppermute x0 -> x2, waiting for transfers between devices: none -> 12 us  [the longest x1 10 us: per_device(): over = lax.ppermute(over, 'node', [(i, (i + 1) % 32) for i in range(32)])]
    scatter-add x1 -> x0, other arithmetic: 12 us -> none  [per_device(): gradient = jnp.zeros(table.shape, jnp.float32).at[local_rows].add(got_grads)]
    dot_general x1 -> x0, matrix products: 11.6 us -> none  [weighted_sums(): lax.dot_general(counts, pooled, (((0,), (0,)), ((), ())), preferred_eleme...]
    all_gather x2 -> x1, blocking collectives: 24.9 us -> 14.2 us  [per_device(): lax.all_gather(packed, 'local', axis=0, tiled=True, axis_index_groups=sam...]
    all_to_all x2 -> x1, starting transfers between devices: 21.8 us -> 11.3 us  [per_device(): lax.all_to_all(codes, 'node', split_axis=0, concat_axis=0, tiled=True)]
  transfers between devices with their start and end apart: 3 -> 3, of which waited for: 1 -> 3; matrix products, arithmetic and copies ran while one was open for 74% -> 0% of each run, Pallas kernels for 0% -> 0%
where the time goes in v1:
time: 70.2 us; the launch traced here: 69.6 us
  Pallas kernels  24 us (34%)
  waiting for transfers between devices  14.7 us (21%)
  blocking collectives  14.2 us (20%)
  starting transfers between devices  13.3 us (19%)
  local copies, waits for them, and re-layouts  2.58 us (4%)
    all_gather x1, blocking collectives, per_device(): lax.all_gather(packed, 'local', axis=0, tiled=True, axis_index_groups=sam...  14.2 us
    pallas_call x1, Pallas kernels, sums(): pl.pallas_call(sums_kernel, out_shape=[jax.ShapeDtypeStruct((128, OWN), F...  12.3 us
    all_to_all x1, starting transfers between devices, per_device(): lax.all_to_all(codes, 'node', split_axis=0, concat_axis=0, tiled=True)  11.3 us
    ppermute x1, waiting for transfers between devices, per_device(): over = lax.ppermute(over, 'node', [(i, (i + 1) % 32) for i in range(32)])  10 us
    pallas_call x1, Pallas kernels, update(): pl.pallas_call(update_kernel, grid=(16,), out_shape=[jax.ShapeDtypeStruct...  10 us
    all_to_all x1, waiting for transfers between devices, per_device(): lax.all_to_all(codes, 'node', split_axis=0, concat_axis=0, tiled=True)  2.75 us
    unnamed x12, local copies, waits for them, and re-layouts  2.58 us
    ppermute x1, waiting for transfers between devices, per_device(): other = lax.ppermute(other, 'local', [(i, i ^ 1) for i in range(8)])  1.99 us
  transfers between devices with their start and end apart: 3, of which 3 were waited for; matrix products, arithmetic and copies ran while one was open for 0% of the time, Pallas kernels for 0%

profile of v1, /device:TPU:24, one launch (start us, length us, event | category | flops | bytes accessed | tf_op | source)
XLA Modules:
  0.0 69.6 jit_solution(16420523751700996944)
XLA Ops:
  0.6 0.0 copy-start
  0.6 0.0 copy-start.1
  0.7 1.0 %copy-done.1 = bf16[512,128]{1,0:T(8,128)(2,1)S(1)} copy-done((bf16[512,128]{1,0:T(8,128)(2,1)S(1)}, bf16[512,128]{1,0:T(8,128)(2,1)}, u32[]{:S(2)}) %copy-start.1) | copy-done | bytes 131096
  1.7 0.0 copy-start.2
  1.7 0.8 %copy-done.2 = s32[512,32]{0,1:T(8,128)S(1)} copy-done((s32[512,32]{0,1:T(8,128)S(1)}, s32[512,32]{0,1:T(8,128)}, u32[]{:S(2)}) %copy-start.2) | copy-done | bytes 65560
  2.5 0.0 copy-start.5
  2.5 0.7 copy-done.5
  3.2 0.0 copy-start.4
  3.2 0.0 copy-start.3
  3.2 0.2 prep.1
  3.4 14.2 %all_gather.3.got_ref = bf16[3072,128]{1,0:T(8,128)(2,1)S(1)} all-gather(bf16[768,128]{1,0:T(8,128)(2,1)S(1)} %prep.1), channel_id=1, replica_groups={{0,2,4,6},{1,3,5,7},{8,10,12,14},{9,11,13,15},{16,18,20,22},{17,19,21,2..., dimensions={0}, use_global_device_ids=true | all-gather | bytes 983040 | tf_op jit(solution)/shard_map/all_gather | solution.py:265
  17.7 0.1 pad_add_fusion.place_ref
  17.7 12.3 %sums.1 = (f32[128,1152]{1,0:T(8,128)S(1)}, f32[128,1152]{1,0:T(8,128)S(1)}) custom-call(s32[3]{0:T(128)S(1)} %pad_add_fusion.place_ref, bf16[3072,128]{1,0:T(8,128)(2,1)S(1)} %all_gather.3.got_ref), custom_call_target="tpu_custom_call" | custom-call | tf_op jit(solution)/shard_map/sums/pallas_call | solution.py:211
  30.0 0.1 collective-permute-start
  30.1 2.0 %collective-permute-done.got_ref = f32[128,1152]{1,0:T(8,128)S(1)} collective-permute-done((f32[128,1152]{1,0:T(8,128)S(1)}, f32[128,1152]{1,0:T(8,128)S(1)}, u32[]{:S(2)}, u32[]{:S(2)}) %collective-permute-start) | collective-permute-done | bytes 589856 | tf_op jit(solution)/shard_map/ppermute | solution.py:267
  32.1 0.0 copy-done.4
  32.1 1.5 %code.1 = (s16[32,40,128]{2,1,0:T(8,128)(2,1)}, s16[80,128]{1,0:T(8,128)(2,1)S(1)}) custom-call(s32[3]{0:T(128)S(1)} %pad_add_fusion.place_ref, f32[128,1152]{1,0:T(8,128)S(1)} %get-tuple-element.8.own_ref, f32[128,1152]{1,0:T(8,128)S(1)} %collective-permute-done.got_ref, s32[16,128]{1,0:T(8,128)S(1)} %bitcast.10), custom_call_target="tpu_custom_call" | custom-call | tf_op jit(solution)/shard_map/code/pallas_call | solution.py:227
  33.6 11.3 %all-to-all-start = ((s16[32,40,128]{2,1,0:T(8,128)(2,1)}), s16[32,40,128]{2,1,0:T(8,128)(2,1)S(1)}, u32[]{:S(2)}, u32[]{:S(2)}) async-start(s16[32,40,128]{2,1,0:T(8,128)(2,1)} %get-tuple-element.10), calls=%async_computation | async-start | bytes 655360 | tf_op jit(solution)/shard_map/all_to_all | solution.py:270
  45.0 1.9 %collective-permute-start.1 = (s16[80,128]{1,0:T(8,128)(2,1)S(1)}, s16[80,128]{1,0:T(8,128)(2,1)S(1)}, u32[]{:S(2)}, u32[]{:S(2)}) collective-permute-start(s16[80,128]{1,0:T(8,128)(2,1)S(1)} %get-tuple-element.11), channel_id=1, source_target_pairs={{0,8},{8,16},{16,24},{24,32},{32,40},{40,48},{48,56},{56,64},{64,7... | collective-permute-start | bytes 61448 | tf_op jit(solution)/shard_map/ppermute | solution.py:269
  46.8 10.0 %collective-permute-done.1.over_ref = s16[80,128]{1,0:T(8,128)(2,1)S(1)} collective-permute-done((s16[80,128]{1,0:T(8,128)(2,1)S(1)}, s16[80,128]{1,0:T(8,128)(2,1)S(1)}, u32[]{:S(2)}, u32[]{:S(2)}) %collective-permute-start.1) | collective-permute-done | bytes 20512 | tf_op jit(solution)/shard_map/ppermute | solution.py:269
  56.8 2.7 %all-to-all-done.got_ref = s16[32,40,128]{2,1,0:T(8,128)(2,1)S(1)} async-done(((s16[32,40,128]{2,1,0:T(8,128)(2,1)}), s16[32,40,128]{2,1,0:T(8,128)(2,1)S(1)}, u32[]{:S(2)}, u32[]{:S(2)}) %all-to-all-start) | async-done | bytes 327712 | tf_op jit(solution)/shard_map/all_to_all | solution.py:270
  59.6 0.0 copy-done
  59.6 0.0 copy-done.3
  59.6 10.0 %update.1 = (f32[4096,128]{1,0:T(8,128)}, f32[32,128]{1,0:T(8,128)}) custom-call(s32[3]{0:T(128)S(1)} %pad_add_fusion.place_ref, s16[32,40,128]{2,1,0:T(8,128)(2,1)S(1)} %all-to-all-done.got_ref, s16[80,128]{1,0:T(8,128)(2,1)S(1)} %collective-permute-done.1.over_ref, f32[4096,128]{1,0:T(8,128)S(1)} %copy-done, f32[32,128]{1,0:T(8,128)S(1)} %bitcast.9), custom_call_target="tpu_custom_call" | custom-call | tf_op jit(solution)/shard_map/update/pallas_call | solution.py:242
Async XLA Ops:
  0.6 59.0 %copy-start = (f32[4096,128]{1,0:T(8,128)S(1)}, f32[4096,128]{1,0:T(8,128)}, u32[]{:S(2)}) copy-start(f32[4096,128]{1,0:T(8,128)} %table_ref.1) | copy-start | bytes 6291460
  0.6 1.1 %copy-start.1 = (bf16[512,128]{1,0:T(8,128)(2,1)S(1)}, bf16[512,128]{1,0:T(8,128)(2,1)}, u32[]{:S(2)}) copy-start(bf16[512,128]{1,0:T(8,128)(2,1)} %pooled_ref.1) | copy-start | bytes 393220
  1.7 0.8 %copy-start.2 = (s32[512,32]{0,1:T(8,128)S(1)}, s32[512,32]{0,1:T(8,128)}, u32[]{:S(2)}) copy-start(s32[512,32]{0,1:T(8,128)} %param.8) | copy-start | bytes 196612
  2.5 0.7 copy-start.5
  3.2 28.9 %copy-start.4 = (s32[2048]{0:T(1024)S(1)}, s32[2048]{0:T(1024)}, u32[]{:S(2)}) copy-start(s32[2048]{0:T(1024)} %param.9) | copy-start | bytes 24580
  3.2 56.4 %copy-start.3 = (f32[4096]{0:T(1024)S(1)}, f32[4096]{0:T(1024)}, u32[]{:S(2)}) copy-start(f32[4096]{0:T(1024)} %param.11) | copy-start | bytes 49156
  30.0 2.1 %collective-permute-start = (f32[128,1152]{1,0:T(8,128)S(1)}, f32[128,1152]{1,0:T(8,128)S(1)}, u32[]{:S(2)}, u32[]{:S(2)}) collective-permute-start(f32[128,1152]{1,0:T(8,128)S(1)} %get-tuple-element.9), channel_id=1, source_target_pairs={{0,1},{1,0},{2,3},{3,2},{4,5},{5,4},{6,7},{7,6},{8,9},{9,8},{10,11... | collective-permute-start | bytes 1769480 | tf_op jit(solution)/shard_map/ppermute | solution.py:267
  33.6 25.9 %all-to-all-start = ((s16[32,40,128]{2,1,0:T(8,128)(2,1)}), s16[32,40,128]{2,1,0:T(8,128)(2,1)S(1)}, u32[]{:S(2)}, u32[]{:S(2)}) async-start(s16[32,40,128]{2,1,0:T(8,128)(2,1)} %get-tuple-element.10), calls=%async_computation | async-start | bytes 655360 | tf_op jit(solution)/shard_map/all_to_all | solution.py:270
  45.0 11.9 %collective-permute-start.1 = (s16[80,128]{1,0:T(8,128)(2,1)S(1)}, s16[80,128]{1,0:T(8,128)(2,1)S(1)}, u32[]{:S(2)}, u32[]{:S(2)}) collective-permute-start(s16[80,128]{1,0:T(8,128)(2,1)S(1)} %get-tuple-element.11), channel_id=1, source_target_pairs={{0,8},{8,16},{16,24},{24,32},{32,40},{40,48},{48,56},{56,64},{64,7... | collective-permute-start | bytes 61448 | tf_op jit(solution)/shard_map/ppermute | solution.py:269

commit v2 on v1

v2 whole, which is shorter than its diff:
```python
import jax
import jax.numpy as jnp
from jax import lax
from jax.experimental import pallas as pl
from jax.experimental.pallas import tpu as pltpu
from jax.sharding import PartitionSpec as P

LEARN_RATE = 0.3
EPSILON = 1e-06

LANES = 128
KEEP = 32
GROUP = 8
BLOCKS = 17
BUCKET_ROWS = 40
F32, BF16, I32 = jnp.float32, jnp.bfloat16, jnp.int32


def rows_iota(rows, cols):
    return lax.broadcasted_iota(I32, (rows, cols), 0)


def lanes_iota(rows, cols):
    return lax.broadcasted_iota(I32, (rows, cols), 1)


def prep_kernel(slot_ref, len_ref, pooled_ref, out_ref, perm_ref):
    slot = slot_ref[...]
    present = rows_iota(*slot.shape) < len_ref[...]
    side = (slot >> 11) & 1
    owner = (slot >> 6) & 31
    place = slot & 63
    first = place < KEEP
    low = jnp.where(first, (owner & 3) * KEEP + place, side * KEEP + place - KEEP)
    low = jnp.where(present, low, -1)
    block = (slot >> 12) * BLOCKS + jnp.where(first, side * 8 + (owner >> 2), 16)

    def by_group(x):
        parts = [x[:, LANES * b : LANES * (b + 1)] for b in range(4)]
        return jnp.concatenate(parts, axis=0).T.astype(BF16)

    out_ref[512:640, :] = by_group(low.astype(F32))
    out_ref[640:768, :] = by_group(block.astype(F32))
    for h in range(2):
        for b in range(4):
            start = b * 128 + h * 64
            perm_ref[pl.ds(h * 4 + b, 64, stride=GROUP), :] = pooled_ref[start : start + 64, :].astype(F32)
    for t in range(4):
        out_ref[t * 128 : (t + 1) * 128, :] = perm_ref[t * 128 : (t + 1) * 128, :].T.astype(BF16)


def sums_kernel(place_ref, got_ref, row_ref, own_ref, other_ref, over_ref, cross_ref, low_ref, code_ref, counts_ref):
    chip, core = place_ref[0], place_ref[1]
    for ch in range(4):
        base = ch * 768
        low_ref[ch * 128 : (ch + 1) * 128, :] = got_ref[base + 512 : base + 640, :].astype(F32)
        block = got_ref[base + 640 : base + 768, :].astype(F32).astype(I32) - chip * BLOCKS
        valid = (block >= 0) & (block < BLOCKS)
        block = jnp.where(block < 16, block ^ (core * 8), block)
        member = (rows_iota(128, 128) >> 6) * 4 + (lanes_iota(128, 128) >> 5)
        code = jnp.where(valid, block * GROUP + member, -1)
        code_ref[ch * 128 : (ch + 1) * 128, :] = code.astype(F32)

    tiles = [(rows_iota(16, 128) + 16 * t).astype(F32).astype(BF16) for t in range(9)]
    one, zero = jnp.ones((16, 128), BF16), jnp.zeros((16, 128), BF16)

    def onehot(ref, row, count):
        halves = []
        for h in range(2):
            line = ref[pl.ds(row + h * 64, 1), :]
            line = jnp.broadcast_to(line, (16, 128)).astype(BF16)
            halves.append(jnp.concatenate([jnp.where(line == tiles[t], one, zero) for t in range(count)], axis=0))
        return jnp.concatenate(halves, axis=1).astype(jnp.float8_e4m3fn)

    def group_counts(row):
        return lax.dot_general(
            onehot(code_ref, row, 9), onehot(low_ref, row, 8), (((1,), (1,)), ((), ())), preferred_element_type=F32
        )

    def step(i, carry):
        ch, pair = i // 32, i % 32
        row = ch * 128 + pair * 2
        first, second = group_counts(row), group_counts(row + 1)
        at = pl.multiple_of(i * 16, 16)
        for b in range(BLOCKS):
            both = jnp.concatenate([first[b * 8 : b * 8 + 8, :], second[b * 8 : b * 8 + 8, :]], axis=0)
            counts_ref[pl.ds(at, 16), b * 128 : (b + 1) * 128] = both.astype(BF16)
        return carry

    lax.fori_loop(0, 128, step, 0, unroll=64)

    pooled = jnp.concatenate(
        [got_ref[ch * 768 + t * 128 : ch * 768 + (t + 1) * 128, :] for ch in range(4) for t in range(4)], axis=1
    )
    total = jnp.dot(pooled, counts_ref[...], preferred_element_type=F32)
    own_ref[...] = total[:, :1024]
    other_ref[...] = total[:, 1024:2048]
    over = total[:, 2048:].T
    near = jnp.broadcast_to(core == 0, (KEEP, LANES))
    over_ref[0:32, :] = jnp.where(near, over[0:32, :], over[32:64, :])
    cross_ref[...] = jnp.where(near, over[32:64, :], over[0:32, :])
    line = row_ref[pl.ds(((place_ref[2] + 1) & 31) >> 1, 1), :] & 4095
    over_ref[32:40, :] = jnp.broadcast_to(line, (8, 128)).astype(F32)


def code_kernel(own_ref, got_ref, row_ref, out_ref):
    rows = row_ref[...] & 4095

    def coded(b):
        total = own_ref[:, b * 128 : (b + 1) * 128] + got_ref[:, b * 128 : (b + 1) * 128]
        most = jnp.max(jnp.abs(total), axis=0, keepdims=True)
        power = jnp.floor(jnp.log2(jnp.maximum(most, 1e-30))) + 1.0
        scaled = jnp.clip(jnp.round(total * jnp.exp2(15.0 - power)), -32767.0, 32767.0)
        return scaled.T.astype(I32).astype(jnp.int16), power.astype(I32)

    def tail(row_line, power_line):
        at = rows_iota(8, 128)
        out = jnp.where(at == 0, jnp.broadcast_to(row_line, (8, 128)), jnp.broadcast_to(power_line, (8, 128)))
        return out

    for b in range(8):
        codes, power = coded(b)
        for q in range(4):
            n = b * 4 + q
            out_ref[n, 0:32, :] = codes[q * 32 : (q + 1) * 32, :]
            out_ref[n, 32:40, :] = tail(rows[n >> 1 : (n >> 1) + 1, :], power).astype(jnp.int16)

def update_kernel(place_ref, got_ref, over_ref, cross_ref, table_ref, accum_ref, table_out, accum_out, value_ref, line_ref, fresh_ref, sems):
    node = place_ref[2]

    def halves(x):
        x = x.astype(I32)
        return (x >> 8).astype(F32).astype(BF16), (x & 255).astype(F32).astype(BF16)

    for m in range(32):
        high, low = halves(got_ref[m, 0:32, :])
        value_ref[m * 32 : (m + 1) * 32, 0:128] = high
        value_ref[m * 32 : (m + 1) * 32, 128:256] = low
    over = over_ref[0:32, :] + cross_ref[...]
    high = (over * (1.0 / 256.0)).astype(BF16)
    rest = over - high.astype(F32) * 256.0
    middle = rest.astype(BF16)
    value_ref[1024:1056, 0:128] = high
    value_ref[1024:1056, 128:256] = middle
    value_ref[1056:1088, 0:128] = jnp.zeros((32, 128), BF16)
    value_ref[1056:1088, 128:256] = (rest - middle.astype(F32)).astype(BF16)
    value_ref[1088:1152, :] = jnp.zeros((64, 256), BF16)

    quarter = lanes_iota(8, 128) >> 5
    ids, powers = jnp.zeros((8, 128), I32), jnp.zeros((8, 128), I32)
    for r in range(4):
        tails = [got_ref[kb * 4 + r, 32:40, :].astype(I32) for kb in range(8)]
        id_lines = jnp.concatenate([t[0:1, :] for t in tails], axis=0)
        power_lines = jnp.concatenate([t[1:2, :] for t in tails], axis=0)
        id_lines = pltpu.roll(id_lines, (r * 32 + 128 - (node & 1) * 64) & 127, axis=1)
        power_lines = pltpu.roll(power_lines, (r * 32 + 128 - (node & 3) * 32) & 127, axis=1)
        ids = jnp.where(quarter == r, id_lines, ids)
        powers = jnp.where(quarter == r, power_lines, powers)
    line_ref[0:8, :] = ids
    line_ref[8:16, :] = powers
    over_line = over_ref[32:40, :].astype(I32)
    first = pltpu.roll(over_line, (128 - ((node & 1) * 64 + 32)) & 127, axis=1)
    second = pltpu.roll(over_line, (128 - (node & 1) * 64) & 127, axis=1)
    lane = lanes_iota(8, 128)
    line_ref[16:24, :] = jnp.where(lane < 32, first, jnp.where(lane < 64, second, -1))

    tiles = [(rows_iota(16, 128) + 16 * t).astype(F32).astype(BF16) for t in range(16)]
    zero = jnp.zeros((16, 128), BF16)
    diag = rows_iota(128, 128) == lanes_iota(128, 128)
    scales = []
    for kb in range(9):
        scale = jnp.ones((1, 128), F32) if kb == 8 else jnp.exp2(line_ref[kb + 8 : kb + 9, :].astype(F32) - 15.0)
        scales.append(jnp.broadcast_to(scale, (16, 128)).astype(BF16))
    values = value_ref[...]

    copies = []
    for p in range(16):
        first_row = p * 256
        parts = []
        for kb in range(9):
            at_id = kb if kb < 8 else 16
            ids = (line_ref[at_id : at_id + 1, :] - first_row).astype(F32)
            ids = jnp.broadcast_to(ids, (16, 128)).astype(BF16)
            parts.append(jnp.concatenate([jnp.where(ids == tiles[t], scales[kb], zero) for t in range(16)], axis=0))
        hot = jnp.concatenate(parts, axis=1)
        both = jnp.dot(hot, values, preferred_element_type=F32)
        gradient = both[:, 0:128] * 256.0 + both[:, 128:256]
        for t in range(2):
            g = gradient[t * 128 : (t + 1) * 128, :]
            line = slice(p * 2 + t, p * 2 + t + 1)
            accum = jnp.broadcast_to(accum_ref[line, :], (128, 128))
            fresh = jnp.sum(g * g * (1.0 / 128.0) + jnp.where(diag, accum, 0.0), axis=1, keepdims=True)
            accum_out[line, :] = jnp.sum(jnp.where(diag, fresh, 0.0), axis=0, keepdims=True)
            step = LEARN_RATE * g / (jnp.sqrt(fresh) + EPSILON)
            at = slice(p * 256 + t * 128, p * 256 + t * 128 + 128)
            fresh_ref[at, :] = table_ref[at, :] - step
        if p % 4 == 3:
            done = pl.ds((p - 3) * 256, 1024)
            copies.append(pltpu.make_async_copy(fresh_ref.at[done, :], table_out.at[done, :], sems.at[p // 4]))
            copies[-1].start()
    for copy in copies:
        copy.wait()


VMEM = pl.BlockSpec(memory_space=pltpu.VMEM)
SMEM = pl.BlockSpec(memory_space=pltpu.SMEM)
PARAMS = pltpu.CompilerParams(vmem_limit_bytes=40 * 1024 * 1024)


def whole(*shape):
    return pl.BlockSpec(shape, lambda i: (0,) * len(shape))


def prep(slot_t, lengths, pooled):
    return pl.pallas_call(
        prep_kernel,
        grid=(1,),
        out_shape=jax.ShapeDtypeStruct((768, 128), BF16),
        in_specs=[whole(32, 512), whole(1, 512), whole(512, 128)],
        out_specs=VMEM,
        scratch_shapes=[pltpu.VMEM((512, 128), F32)],
        compiler_params=pltpu.CompilerParams(vmem_limit_bytes=63 * 1024 * 1024),
        name="prep",
    )(slot_t, lengths, pooled)


def sums(place, got, slot_row):
    return pl.pallas_call(
        sums_kernel,
        out_shape=[
            jax.ShapeDtypeStruct((128, 1024), F32),
            jax.ShapeDtypeStruct((128, 1024), F32),
            jax.ShapeDtypeStruct((40, 128), F32),
            jax.ShapeDtypeStruct((32, 128), F32),
        ],
        in_specs=[SMEM, VMEM, VMEM],
        out_specs=[VMEM] * 4,
        scratch_shapes=[
            pltpu.VMEM((512, 128), F32),
            pltpu.VMEM((512, 128), F32),
            pltpu.VMEM((2048, BLOCKS * 128), BF16),
        ],
        compiler_params=PARAMS,
        name="sums",
    )(place, got, slot_row)


def code(own, got, slot_row):
    return pl.pallas_call(
        code_kernel,
        out_shape=jax.ShapeDtypeStruct((32, BUCKET_ROWS, 128), jnp.int16),
        in_specs=[VMEM] * 3,
        out_specs=VMEM,
        compiler_params=PARAMS,
        name="code",
    )(own, got, slot_row)


def update(place, got, over, cross, table, accum):
    return pl.pallas_call(
        update_kernel,
        out_shape=[jax.ShapeDtypeStruct((4096, 128), F32), jax.ShapeDtypeStruct((32, 128), F32)],
        in_specs=[SMEM] + [VMEM] * 5,
        out_specs=[pl.BlockSpec(memory_space=pl.ANY), VMEM],
        scratch_shapes=[
            pltpu.VMEM((1152, 256), BF16),
            pltpu.VMEM((24, 128), I32),
            pltpu.VMEM((4096, 128), F32),
            pltpu.SemaphoreType.DMA((4,)),
        ],
        compiler_params=PARAMS,
        name="update",
    )(place, got, over, cross, table, accum)


def next_node(flip):
    return [(n * 8 + i, (n + 1) % 32 * 8 + (i ^ flip)) for n in range(32) for i in range(8)]


def per_device(pooled_grad, lengths, slot_of, slot_row, table, accum):
    local, node = lax.axis_index("local"), lax.axis_index("node")
    place = jnp.stack([local >> 1, local & 1, node]).astype(I32)
    packed = prep(slot_of.T, lengths.reshape(1, 512), pooled_grad)
    same_core = [[0, 2, 4, 6], [1, 3, 5, 7]]
    got = lax.all_gather(packed, "local", axis=0, tiled=True, axis_index_groups=same_core)
    rows = slot_row.reshape(16, 128)
    own, other, over, cross = sums(place, got, rows)
    other = lax.ppermute(other, "local", [(i, i ^ 1) for i in range(8)])
    over = lax.ppermute(over, ("node", "local"), next_node(0))
    cross = lax.ppermute(cross, ("node", "local"), next_node(1))
    codes = lax.all_to_all(code(own, other, rows), "node", split_axis=0, concat_axis=0, tiled=True)
    table_new, accum_new = update(place, codes, over, cross, table, accum.reshape(32, 128))
    return table_new, accum_new.reshape(4096)


def solution(mesh):
    return jax.shard_map(
        per_device,
        mesh=mesh,
        in_specs=(
            P(("node", "local"), None),
            P(("node", "local")),
            P(("node", "local"), None),
            P(("node", "local")),
            P(("node", "local"), None),
            P(("node", "local")),
        ),
        out_specs=(P(("node", "local"), None), P(("node", "local"))),
        check_vma=False,
    )
```

time: 70.2 us -> 58.3 us (0.83)
  Pallas kernels: 24 us -> 13.7 us
  local copies, waits for them, and re-layouts: 2.58 us -> 0.71 us
    pallas_call x4, Pallas kernels: 24 us -> 13.7 us  [the longest x1 5.71 us: sums(): pl.pallas_call(sums_kernel, out_shape=[jax.ShapeDtypeStruct((128, 1024),...]
    unnamed x12 -> x6, local copies, waits for them, and re-layouts: 2.58 us -> 0.71 us
    ppermute x1 -> x2, starting transfers between devices: 1.87 us -> 2.23 us  [the longest x1 1.87 us: per_device(): over = lax.ppermute(over, ('node', 'local'), next_node(0))]
    ppermute x1 -> x2, waiting for transfers between devices: 10 us -> 9.95 us  [the longest x1 8.27 us: per_device(): cross = lax.ppermute(cross, ('node', 'local'), next_node(1))]
  transfers between devices with their start and end apart: 3 -> 4, of which waited for: 3 -> 4; matrix products, arithmetic and copies ran while one was open for 0% -> 0% of each run, Pallas kernels for 0% -> 0%
where the time goes in v2:
time: 58.3 us; the launch traced here: 57.8 us
  blocking collectives  14.6 us (25%)
  waiting for transfers between devices  14.5 us (25%)
  Pallas kernels  13.7 us (23%)
  starting transfers between devices  13.6 us (23%)
  local copies, waits for them, and re-layouts  0.71 us (1%)
  between operations  0.67 us (1%)
    all_gather x1, blocking collectives, per_device(): lax.all_gather(packed, 'local', axis=0, tiled=True, axis_index_groups=sam...  14.6 us
    all_to_all x1, starting transfers between devices, per_device(): lax.all_to_all(code(own, other, rows), 'node', split_axis=0, concat_axis=...  11.3 us
    ppermute x1, waiting for transfers between devices, per_device(): cross = lax.ppermute(cross, ('node', 'local'), next_node(1))  8.27 us
    pallas_call x1, Pallas kernels, sums(): pl.pallas_call(sums_kernel, out_shape=[jax.ShapeDtypeStruct((128, 1024),...  5.71 us
    pallas_call x1, Pallas kernels, update(): pl.pallas_call(update_kernel, out_shape=[jax.ShapeDtypeStruct((4096, 128)...  5.17 us
    all_to_all x1, waiting for transfers between devices, per_device(): lax.all_to_all(code(own, other, rows), 'node', split_axis=0, concat_axis=...  2.63 us
    ppermute x1, waiting for transfers between devices, per_device(): other = lax.ppermute(other, 'local', [(i, i ^ 1) for i in range(8)])  1.9 us
    ppermute x1, starting transfers between devices, per_device(): over = lax.ppermute(over, ('node', 'local'), next_node(0))  1.87 us
  transfers between devices with their start and end apart: 4, of which 4 were waited for; matrix products, arithmetic and copies ran while one was open for 0% of the time, Pallas kernels for 0%

profile of v2, /device:TPU:24, one launch (start us, length us, event | category | flops | bytes accessed | tf_op | source)
XLA Modules:
  0.0 57.8 jit_solution(8980859546639780027)
XLA Ops:
  0.6 0.0 copy-start.2
  0.6 1.8 %prep.1 = bf16[768,128]{1,0:T(8,128)(2,1)} custom-call(s32[32,512]{1,0:T(8,128)} %bitcast.11, s32[1,512]{1,0:T(1,128)} %bitcast.12, bf16[512,128]{1,0:T(8,128)(2,1)} %pooled_ref.1), custom_call_target="tpu_custom_call" | custom-call | tf_op jit(solution)/shard_map/prep/pallas_call | solution.py:215
  2.5 0.0 copy-start
  2.5 14.6 %all_gather.3.got_ref = bf16[3072,128]{1,0:T(8,128)(2,1)S(1)} all-gather(bf16[768,128]{1,0:T(8,128)(2,1)} %prep.1), channel_id=1, replica_groups={{0,2,4,6},{1,3,5,7},{8,10,12,14},{9,11,13,15},{16,18,20,22},{17,19,21,2..., dimensions={0}, use_global_device_ids=true | all-gather | bytes 983040 | tf_op jit(solution)/shard_map/all_gather | solution.py:285
  17.1 0.1 pad_add_fusion.place_ref
  17.1 0.0 copy-start.1
  17.1 0.7 %copy-done.1 = s32[2048]{0:T(1024)S(1)} copy-done((s32[2048]{0:T(1024)S(1)}, s32[2048]{0:T(1024)}, u32[]{:S(2)}) %copy-start.1) | copy-done | bytes 8216
  17.8 5.7 %sums.1 = (f32[128,1024]{1,0:T(8,128)S(1)}, f32[128,1024]{1,0:T(8,128)S(1)}, f32[40,128]{1,0:T(8,128)S(1)}, f32[32,128]{1,0:T(8,128)S(1)}) custom-call(s32[3]{0:T(128)S(1)} %pad_add_fusion.place_ref, bf16[3072,128]{1,0:T(8,128)(2,1)S(1)} %all_gather.3.got_ref, s32[16,128]{1,0:T(8,128)S(1)} %bitcast.8), custom_call_target="tpu_custom_call" | custom-call | tf_op jit(solution)/shard_map/sums/pallas_call | solution.py:228
  23.5 0.1 collective-permute-start
  23.6 1.9 %collective-permute-done.got_ref = f32[128,1024]{1,0:T(8,128)S(1)} collective-permute-done((f32[128,1024]{1,0:T(8,128)S(1)}, f32[128,1024]{1,0:T(8,128)S(1)}, u32[]{:S(2)}, u32[]{:S(2)}) %collective-permute-start) | collective-permute-done | bytes 524320 | tf_op jit(solution)/shard_map/ppermute | solution.py:288
  25.5 1.0 %code.1 = s16[32,40,128]{2,1,0:T(8,128)(2,1)} custom-call(f32[128,1024]{1,0:T(8,128)S(1)} %get-tuple-element.8.own_ref, f32[128,1024]{1,0:T(8,128)S(1)} %collective-permute-done.got_ref, s32[16,128]{1,0:T(8,128)S(1)} %bitcast.9), custom_call_target="tpu_custom_call" | custom-call | tf_op jit(solution)/shard_map/code/pallas_call | solution.py:249
  26.5 11.3 %all-to-all-start = ((s16[32,40,128]{2,1,0:T(8,128)(2,1)}), s16[32,40,128]{2,1,0:T(8,128)(2,1)S(1)}, u32[]{:S(2)}, u32[]{:S(2)}) async-start(s16[32,40,128]{2,1,0:T(8,128)(2,1)} %code.1), calls=%async_computation | async-start | bytes 655360 | tf_op jit(solution)/shard_map/all_to_all | solution.py:291
  37.8 1.9 %collective-permute-start.1 = (f32[40,128]{1,0:T(8,128)S(1)}, f32[40,128]{1,0:T(8,128)S(1)}, u32[]{:S(2)}, u32[]{:S(2)}) collective-permute-start(f32[40,128]{1,0:T(8,128)S(1)} %get-tuple-element.10), channel_id=1, source_target_pairs={{0,8},{1,9},{2,10},{3,11},{4,12},{5,13},{6,14},{7,15},{8,16},{9,17... | collective-permute-start | bytes 61448 | tf_op jit(solution)/shard_map/ppermute | solution.py:289
  39.7 0.4 collective-permute-start.2
  40.1 8.3 %collective-permute-done.2.cross_ref = f32[32,128]{1,0:T(8,128)S(1)} collective-permute-done((f32[32,128]{1,0:T(8,128)S(1)}, f32[32,128]{1,0:T(8,128)S(1)}, u32[]{:S(2)}, u32[]{:S(2)}) %collective-permute-start.2) | collective-permute-done | bytes 16416 | tf_op jit(solution)/shard_map/ppermute | solution.py:290
  48.3 1.7 %collective-permute-done.1.over_ref = f32[40,128]{1,0:T(8,128)S(1)} collective-permute-done((f32[40,128]{1,0:T(8,128)S(1)}, f32[40,128]{1,0:T(8,128)S(1)}, u32[]{:S(2)}, u32[]{:S(2)}) %collective-permute-start.1) | collective-permute-done | bytes 20512 | tf_op jit(solution)/shard_map/ppermute | solution.py:289
  50.0 2.6 %all-to-all-done.got_ref = s16[32,40,128]{2,1,0:T(8,128)(2,1)S(1)} async-done(((s16[32,40,128]{2,1,0:T(8,128)(2,1)}), s16[32,40,128]{2,1,0:T(8,128)(2,1)S(1)}, u32[]{:S(2)}, u32[]{:S(2)}) %all-to-all-start) | async-done | bytes 327712 | tf_op jit(solution)/shard_map/all_to_all | solution.py:291
  52.6 0.0 copy-done.2
  52.7 0.0 copy-done
  52.7 5.2 %update.1 = (f32[4096,128]{1,0:T(8,128)}, f32[32,128]{1,0:T(8,128)}) custom-call(s32[3]{0:T(128)S(1)} %pad_add_fusion.place_ref, s16[32,40,128]{2,1,0:T(8,128)(2,1)S(1)} %all-to-all-done.got_ref, f32[40,128]{1,0:T(8,128)S(1)} %collective-permute-done.1.over_ref, f32[32,128]{1,0:T(8,128)S(1)} %collective-permute-done.2.cross_ref, f32[4096,128]{1,0:T(8,128)S(1)} %copy-done, ...), custom_call_target="tpu_custom_call" | custom-call | tf_op jit(solution)/shard_map/update/pallas_call | solution.py:260
Async XLA Ops:
  0.6 52.0 %copy-start.2 = (f32[4096]{0:T(1024)S(1)}, f32[4096]{0:T(1024)}, u32[]{:S(2)}) copy-start(f32[4096]{0:T(1024)} %param.11) | copy-start | bytes 49156
  2.5 50.2 %copy-start = (f32[4096,128]{1,0:T(8,128)S(1)}, f32[4096,128]{1,0:T(8,128)}, u32[]{:S(2)}) copy-start(f32[4096,128]{1,0:T(8,128)} %table_ref.1) | copy-start | bytes 6291460
  17.1 0.7 %copy-start.1 = (s32[2048]{0:T(1024)S(1)}, s32[2048]{0:T(1024)}, u32[]{:S(2)}) copy-start(s32[2048]{0:T(1024)} %param.9) | copy-start | bytes 24580
  23.5 2.0 %collective-permute-start = (f32[128,1024]{1,0:T(8,128)S(1)}, f32[128,1024]{1,0:T(8,128)S(1)}, u32[]{:S(2)}, u32[]{:S(2)}) collective-permute-start(f32[128,1024]{1,0:T(8,128)S(1)} %get-tuple-element.9), channel_id=1, source_target_pairs={{0,1},{1,0},{2,3},{3,2},{4,5},{5,4},{6,7},{7,6},{8,9},{9,8},{10,11... | collective-permute-start | bytes 1572872 | tf_op jit(solution)/shard_map/ppermute | solution.py:288
  26.5 26.1 %all-to-all-start = ((s16[32,40,128]{2,1,0:T(8,128)(2,1)}), s16[32,40,128]{2,1,0:T(8,128)(2,1)S(1)}, u32[]{:S(2)}, u32[]{:S(2)}) async-start(s16[32,40,128]{2,1,0:T(8,128)(2,1)} %code.1), calls=%async_computation | async-start | bytes 655360 | tf_op jit(solution)/shard_map/all_to_all | solution.py:291
  37.8 12.2 %collective-permute-start.1 = (f32[40,128]{1,0:T(8,128)S(1)}, f32[40,128]{1,0:T(8,128)S(1)}, u32[]{:S(2)}, u32[]{:S(2)}) collective-permute-start(f32[40,128]{1,0:T(8,128)S(1)} %get-tuple-element.10), channel_id=1, source_target_pairs={{0,8},{1,9},{2,10},{3,11},{4,12},{5,13},{6,14},{7,15},{8,16},{9,17... | collective-permute-start | bytes 61448 | tf_op jit(solution)/shard_map/ppermute | solution.py:289
  39.7 8.6 %collective-permute-start.2 = (f32[32,128]{1,0:T(8,128)S(1)}, f32[32,128]{1,0:T(8,128)S(1)}, u32[]{:S(2)}, u32[]{:S(2)}) collective-permute-start(f32[32,128]{1,0:T(8,128)S(1)} %get-tuple-element.11), channel_id=1, source_target_pairs={{0,9},{1,8},{2,11},{3,10},{4,13},{5,12},{6,15},{7,14},{8,17},{9,16... | collective-permute-start | bytes 49160 | tf_op jit(solution)/shard_map/ppermute | solution.py:290

commit v3 on v2

--- a/solution.py
+++ b/solution.py
@@ -12,6 +12,7 @@
 KEEP = 32
 GROUP = 8
 BLOCKS = 17
+WIDTH = BLOCKS * LANES
 BUCKET_ROWS = 40
 F32, BF16, I32 = jnp.float32, jnp.bfloat16, jnp.int32
 
@@ -32,15 +33,14 @@
     place = slot & 63
     first = place < KEEP
     low = jnp.where(first, (owner & 3) * KEEP + place, side * KEEP + place - KEEP)
-    low = jnp.where(present, low, -1)
     block = (slot >> 12) * BLOCKS + jnp.where(first, side * 8 + (owner >> 2), 16)
 
     def by_group(x):
         parts = [x[:, LANES * b : LANES * (b + 1)] for b in range(4)]
         return jnp.concatenate(parts, axis=0).T.astype(BF16)
 
-    out_ref[512:640, :] = by_group(low.astype(F32))
-    out_ref[640:768, :] = by_group(block.astype(F32))
+    mark = (1.0 + low.astype(F32) * (1.0 / 128.0)) * jnp.exp2((block - 34).astype(F32))
+    out_ref[512:640, :] = by_group(jnp.where(present, mark, 0.0))
     for h in range(2):
         for b in range(4):
             start = b * 128 + h * 64
@@ -49,17 +49,18 @@
         out_ref[t * 128 : (t + 1) * 128, :] = perm_ref[t * 128 : (t + 1) * 128, :].T.astype(BF16)
 
 
-def sums_kernel(place_ref, got_ref, row_ref, own_ref, other_ref, over_ref, cross_ref, low_ref, code_ref, counts_ref):
+def add_sums(place_ref, pieces, low_ref, code_ref, counts_ref):
     chip, core = place_ref[0], place_ref[1]
-    for ch in range(4):
-        base = ch * 768
-        low_ref[ch * 128 : (ch + 1) * 128, :] = got_ref[base + 512 : base + 640, :].astype(F32)
-        block = got_ref[base + 640 : base + 768, :].astype(F32).astype(I32) - chip * BLOCKS
-        valid = (block >= 0) & (block < BLOCKS)
+    span = jnp.where(chip == 0, 2.0**34, jnp.where(chip == 1, 2.0**17, jnp.where(chip == 2, 1.0, 2.0**-17))).astype(F32)
+    for i, piece in enumerate(pieces):
+        mark = piece(512, 640).astype(F32) * span
+        valid = (mark >= 1.0) & (mark < 2.0**BLOCKS)
+        power = jnp.floor(jnp.log2(jnp.maximum(mark, 0.5)) + 0.002)
+        low_ref[i * 128 : (i + 1) * 128, :] = jnp.round((mark * jnp.exp2(-power) - 1.0) * 128.0)
+        block = jnp.clip(power, 0.0, 16.0).astype(I32)
         block = jnp.where(block < 16, block ^ (core * 8), block)
         member = (rows_iota(128, 128) >> 6) * 4 + (lanes_iota(128, 128) >> 5)
-        code = jnp.where(valid, block * GROUP + member, -1)
-        code_ref[ch * 128 : (ch + 1) * 128, :] = code.astype(F32)
+        code_ref[i * 128 : (i + 1) * 128, :] = jnp.where(valid, block * GROUP + member, -1).astype(F32)
 
     tiles = [(rows_iota(16, 128) + 16 * t).astype(F32).astype(BF16) for t in range(9)]
     one, zero = jnp.ones((16, 128), BF16), jnp.zeros((16, 128), BF16)
@@ -78,8 +79,7 @@
         )
 
     def step(i, carry):
-        ch, pair = i // 32, i % 32
-        row = ch * 128 + pair * 2
+        row = (i // 32) * 128 + (i % 32) * 2
         first, second = group_counts(row), group_counts(row + 1)
         at = pl.multiple_of(i * 16, 16)
         for b in range(BLOCKS):
@@ -87,16 +87,32 @@
             counts_ref[pl.ds(at, 16), b * 128 : (b + 1) * 128] = both.astype(BF16)
         return carry
 
-    lax.fori_loop(0, 128, step, 0, unroll=64)
-
-    pooled = jnp.concatenate(
-        [got_ref[ch * 768 + t * 128 : ch * 768 + (t + 1) * 128, :] for ch in range(4) for t in range(4)], axis=1
-    )
-    total = jnp.dot(pooled, counts_ref[...], preferred_element_type=F32)
+    lax.fori_loop(0, 32 * len(pieces), step, 0, unroll=32)
+    pooled = jnp.concatenate([piece(t * 128, t * 128 + 128) for piece in pieces for t in range(4)], axis=1)
+    return jnp.dot(pooled, counts_ref[...], preferred_element_type=F32)
+
+
+def rows_of(ref):
+    return lambda a, b: ref[a:b, :]
+
+
+def own_kernel(place_ref, mine_ref, total_ref, low_ref, code_ref, counts_ref):
+    total_ref[...] = add_sums(place_ref, [rows_of(mine_ref)], low_ref, code_ref, counts_ref)
+
+
+def near_kernel(place_ref, left_ref, right_ref, before_ref, total_ref, low_ref, code_ref, counts_ref):
+    pieces = [rows_of(left_ref), rows_of(right_ref)]
+    total_ref[...] = before_ref[...] + add_sums(place_ref, pieces, low_ref, code_ref, counts_ref)
+
+
+def far_kernel(place_ref, top_ref, bottom_ref, before_ref, row_ref, own_ref, other_ref, over_ref, cross_ref, low_ref, code_ref, counts_ref, far_ref):
+    far_ref[0:320, :] = top_ref[...]
+    far_ref[320:640, :] = bottom_ref[...]
+    total = before_ref[...] + add_sums(place_ref, [rows_of(far_ref)], low_ref, code_ref, counts_ref)
     own_ref[...] = total[:, :1024]
     other_ref[...] = total[:, 1024:2048]
     over = total[:, 2048:].T
-    near = jnp.broadcast_to(core == 0, (KEEP, LANES))
+    near = jnp.broadcast_to(place_ref[1] == 0, (KEEP, LANES))
     over_ref[0:32, :] = jnp.where(near, over[0:32, :], over[32:64, :])
     cross_ref[...] = jnp.where(near, over[32:64, :], over[0:32, :])
     line = row_ref[pl.ds(((place_ref[2] + 1) & 31) >> 1, 1), :] & 4095
@@ -215,7 +231,7 @@
     return pl.pallas_call(
         prep_kernel,
         grid=(1,),
-        out_shape=jax.ShapeDtypeStruct((768, 128), BF16),
+        out_shape=jax.ShapeDtypeStruct((640, 128), BF16),
         in_specs=[whole(32, 512), whole(1, 512), whole(512, 128)],
         out_specs=VMEM,
         scratch_shapes=[pltpu.VMEM((512, 128), F32)],
@@ -224,25 +240,33 @@
     )(slot_t, lengths, pooled)
 
 
-def sums(place, got, slot_row):
+def sums_call(kernel, name, pieces, outs, extra, *args):
     return pl.pallas_call(
-        sums_kernel,
-        out_shape=[
-            jax.ShapeDtypeStruct((128, 1024), F32),
-            jax.ShapeDtypeStruct((128, 1024), F32),
-            jax.ShapeDtypeStruct((40, 128), F32),
-            jax.ShapeDtypeStruct((32, 128), F32),
-        ],
-        in_specs=[SMEM, VMEM, VMEM],
-        out_specs=[VMEM] * 4,
+        kernel,
+        out_shape=[jax.ShapeDtypeStruct(shape, F32) for shape in outs],
+        in_specs=[SMEM] + [VMEM] * (len(args) - 1),
+        out_specs=[VMEM] * len(outs),
         scratch_shapes=[
-            pltpu.VMEM((512, 128), F32),
-            pltpu.VMEM((512, 128), F32),
-            pltpu.VMEM((2048, BLOCKS * 128), BF16),
-        ],
+            pltpu.VMEM((128 * pieces, 128), F32),
+            pltpu.VMEM((128 * pieces, 128), F32),
+            pltpu.VMEM((512 * pieces, BLOCKS * 128), BF16),
+        ]
+        + extra,
         compiler_params=PARAMS,
-        name="sums",
-    )(place, got, slot_row)
+        cost_estimate=pl.CostEstimate(flops=2_000_000_000 * pieces, bytes_accessed=3_000_000, transcendentals=0),
+        name=name,
+    )(*args)
+
+
+def gather_sums(place, packed, rows):
+    shift = lambda x, k: lax.ppermute(x, "local", [(i, (i + k) % 8) for i in range(8)])
+    left, right = shift(packed, 2), shift(packed, 6)
+    (total,) = sums_call(own_kernel, "own_sums", 1, [(128, WIDTH)], [], place, packed)
+    left, right, total = lax.optimization_barrier((left, right, total))
+    top, bottom = shift(left[:320], 2), shift(right[320:], 6)
+    (total,) = sums_call(near_kernel, "near_sums", 2, [(128, WIDTH)], [], place, left, right, total)
+    outs = [(128, 1024), (128, 1024), (40, 128), (32, 128)]
+    return sums_call(far_kernel, "far_sums", 1, outs, [pltpu.VMEM((640, 128), BF16)], place, top, bottom, total, rows)
 
 
 def code(own, got, slot_row):
@@ -281,14 +305,13 @@
     local, node = lax.axis_index("local"), lax.axis_index("node")
     place = jnp.stack([local >> 1, local & 1, node]).astype(I32)
     packed = prep(slot_of.T, lengths.reshape(1, 512), pooled_grad)
-    same_core = [[0, 2, 4, 6], [1, 3, 5, 7]]
-    got = lax.all_gather(packed, "local", axis=0, tiled=True, axis_index_groups=same_core)
     rows = slot_row.reshape(16, 128)
-    own, other, over, cross = sums(place, got, rows)
+    own, other, over, cross = gather_sums(place, packed, rows)
     other = lax.ppermute(other, "local", [(i, i ^ 1) for i in range(8)])
     over = lax.ppermute(over, ("node", "local"), next_node(0))
     cross = lax.ppermute(cross, ("node", "local"), next_node(1))
-    codes = lax.all_to_all(code(own, other, rows), "node", split_axis=0, concat_axis=0, tiled=True)
+    codes, over, cross = lax.optimization_barrier((code(own, other, rows), over, cross))
+    codes = lax.all_to_all(codes, "node", split_axis=0, concat_axis=0, tiled=True)
     table_new, accum_new = update(place, codes, over, cross, table, accum.reshape(32, 128))
     return table_new, accum_new.reshape(4096)
 

time: 58.3 us -> 57.4 us (0.985)
  blocking collectives: 14.6 us -> 21.2 us
  starting transfers between devices: 13.6 us -> 9.17 us
  waiting for transfers between devices: 14.5 us -> 10.2 us
  Pallas kernels: 13.7 us -> 14.8 us
    all_to_all x0 -> x1, blocking collectives: none -> 21.2 us  [per_device(): lax.all_to_all(codes, 'node', split_axis=0, concat_axis=0, tiled=True)]
    all_gather x1 -> x0, blocking collectives: 14.6 us -> none  [per_device(): lax.all_gather(packed, 'local', axis=0, tiled=True, axis_index_groups=sam...]
    all_to_all x1 -> x0, starting transfers between devices: 11.3 us -> none  [per_device(): lax.all_to_all(code(own, other, rows), 'node', split_axis=0, concat_axis=...]
    ppermute x0 -> x4, starting transfers between devices: none -> 6.26 us  [gather_sums(): lax.ppermute(x, 'local', [(i, (i + k) % 8) for i in range(8)])]
    ppermute x0 -> x4, waiting for transfers between devices: none -> 3.29 us  [gather_sums(): lax.ppermute(x, 'local', [(i, (i + k) % 8) for i in range(8)])]
    all_to_all x1 -> x0, waiting for transfers between devices: 2.63 us -> none  [per_device(): lax.all_to_all(code(own, other, rows), 'node', split_axis=0, concat_axis=...]
    ppermute x1, waiting for transfers between devices: 1.9 us -> 0.01 us  [per_device(): other = lax.ppermute(other, 'local', [(i, i ^ 1) for i in range(8)])]
    pallas_call x2 -> x4, Pallas kernels: 7.54 us -> 9.39 us  [the longest x3 7.57 us: sums_call(): pl.pallas_call(kernel, out_shape=[jax.ShapeDtypeStruct(shape, F32) for sh...]
  transfers between devices with their start and end apart: 4 -> 7, of which waited for: 4 -> 4; matrix products, arithmetic and copies ran while one was open for 0% -> 0% of each run, Pallas kernels for 0% -> 10%
where the time goes in v3:
time: 57.4 us; the launch traced here: 57.3 us
  blocking collectives  21.2 us (37%)
  Pallas kernels  14.8 us (26%)
  waiting for transfers between devices  10.2 us (18%)
  starting transfers between devices  9.17 us (16%)
  local copies, waits for them, and re-layouts  0.94 us (2%)
  between operations  0.86 us (1%)
    all_to_all x1, blocking collectives, per_device(): lax.all_to_all(codes, 'node', split_axis=0, concat_axis=0, tiled=True)  21.2 us
    pallas_call x3, Pallas kernels, sums_call(): pl.pallas_call(kernel, out_shape=[jax.ShapeDtypeStruct(shape, F32) for sh...  7.57 us
    ppermute x1, waiting for transfers between devices, per_device(): cross = lax.ppermute(cross, ('node', 'local'), next_node(1))  6.82 us
    ppermute x4, starting transfers between devices, gather_sums(): lax.ppermute(x, 'local', [(i, (i + k) % 8) for i in range(8)])  6.26 us
    pallas_call x1, Pallas kernels, update(): pl.pallas_call(update_kernel, out_shape=[jax.ShapeDtypeStruct((4096, 128)...  5.16 us
    ppermute x4, waiting for transfers between devices, gather_sums(): lax.ppermute(x, 'local', [(i, (i + k) % 8) for i in range(8)])  3.29 us
    pallas_call x1, Pallas kernels, prep(): pl.pallas_call(prep_kernel, grid=(1,), out_shape=jax.ShapeDtypeStruct((64...  1.82 us
    ppermute x1, starting transfers between devices, per_device(): over = lax.ppermute(over, ('node', 'local'), next_node(0))  1.57 us
  transfers between devices with their start and end apart: 7, of which 4 were waited for; matrix products, arithmetic and copies ran while one was open for 0% of the time, Pallas kernels for 10%

profile of v3, /device:TPU:24, one launch (start us, length us, event | category | flops | bytes accessed | tf_op | source)
XLA Modules:
  0.0 57.3 jit_solution(5445688874315271290)
XLA Ops:
  0.6 1.8 %prep.1.mine_ref = bf16[640,128]{1,0:T(8,128)(2,1)} custom-call(s32[32,512]{1,0:T(8,128)} %bitcast.11, s32[1,512]{1,0:T(1,128)} %bitcast.12, bf16[512,128]{1,0:T(8,128)(2,1)} %pooled_ref.1), custom_call_target="tpu_custom_call" | custom-call | tf_op jit(solution)/shard_map/prep/pallas_call | solution.py:231
  2.5 0.7 %collective-permute-start.1 = (bf16[640,128]{1,0:T(8,128)(2,1)}, bf16[640,128]{1,0:T(8,128)(2,1)S(1)}, u32[]{:S(2)}, u32[]{:S(2)}) collective-permute-start(bf16[640,128]{1,0:T(8,128)(2,1)} %prep.1.mine_ref), channel_id=1, source_target_pairs={{0,6},{1,7},{2,0},{3,1},{4,2},{5,3},{6,4},{7,5},{8,14},{9,15},{10,... | collective-permute-start | bytes 491528 | tf_op jit(solution)/shard_map/ppermute | solution.py:262
  3.2 2.5 %collective-permute-start = (bf16[640,128]{1,0:T(8,128)(2,1)}, bf16[640,128]{1,0:T(8,128)(2,1)S(1)}, u32[]{:S(2)}, u32[]{:S(2)}) collective-permute-start(bf16[640,128]{1,0:T(8,128)(2,1)} %prep.1.mine_ref), channel_id=1, source_target_pairs={{0,2},{1,3},{2,4},{3,5},{4,6},{5,7},{6,0},{7,1},{8,10},{9,11},{10,... | collective-permute-start | bytes 491528 | tf_op jit(solution)/shard_map/ppermute | solution.py:262
  5.7 0.1 pad_add_fusion.place_ref
  5.8 0.0 copy-start.1
  5.8 0.9 %copy-done.1 = bf16[640,128]{1,0:T(8,128)(2,1)S(1)} copy-done((bf16[640,128]{1,0:T(8,128)(2,1)S(1)}, bf16[640,128]{1,0:T(8,128)(2,1)}, u32[]{:S(2)}) %copy-start.1) | copy-done | bytes 163864
  6.7 2.0 %own_sums.1.before_ref = f32[128,2176]{1,0:T(8,128)S(1)} custom-call(s32[3]{0:T(128)S(1)} %pad_add_fusion.place_ref, bf16[640,128]{1,0:T(8,128)(2,1)S(1)} %copy-done.1), custom_call_target="tpu_custom_call" | custom-call | flops 2000000000 | bytes 3000000 | tf_op jit(solution)/shard_map/own_sums/pallas_call | solution.py:244
  8.7 1.1 %collective-permute-done.1.right_ref = bf16[640,128]{1,0:T(8,128)(2,1)S(1)} collective-permute-done((bf16[640,128]{1,0:T(8,128)(2,1)}, bf16[640,128]{1,0:T(8,128)(2,1)S(1)}, u32[]{:S(2)}, u32[]{:S(2)}) %collective-permute-start.1) | collective-permute-done | bytes 163872 | tf_op jit(solution)/shard_map/ppermute | solution.py:262
  9.8 0.0 collective-permute-done.left_ref
  9.8 0.0 copy-start.3
  9.9 3.0 %collective-permute-start.2 = (bf16[320,128]{1,0:T(8,128)(2,1)S(1)}, bf16[320,128]{1,0:T(8,128)(2,1)S(1)}, u32[]{:S(2)}, u32[]{:S(2)}) collective-permute-start(bf16[320,128]{1,0:T(8,128)(2,1)S(1)} %slice.6), channel_id=1, source_target_pairs={{0,2},{1,3},{2,4},{3,5},{4,6},{5,7},{6,0},{7,1},{8,10},{9,11},{10,... | collective-permute-start | bytes 245768 | tf_op jit(solution)/shard_map/ppermute | solution.py:262
  12.9 0.0 collective-permute-start.3
  12.9 3.4 %near_sums.1.before_ref = f32[128,2176]{1,0:T(8,128)S(1)} custom-call(s32[3]{0:T(128)S(1)} %pad_add_fusion.place_ref, bf16[640,128]{1,0:T(8,128)(2,1)S(1)} %collective-permute-done.left_ref, bf16[640,128]{1,0:T(8,128)(2,1)S(1)} %collective-permute-done.1.right_ref, f32[128,2176]{1,0:T(8,128)S(1)} %own_sums.1.before_ref), custom_call_target="tpu_custom_call" | custom-call | flops 4000000000 | bytes 3000000 | tf_op jit(solution)/shard_map/near_sums/pallas_call | solution.py:244
  16.3 0.0 collective-permute-done.2.top_ref
  16.3 2.2 %collective-permute-done.3.bottom_ref = bf16[320,128]{1,0:T(8,128)(2,1)S(1)} collective-permute-done((bf16[320,128]{1,0:T(8,128)(2,1)S(1)}, bf16[320,128]{1,0:T(8,128)(2,1)S(1)}, u32[]{:S(2)}, u32[]{:S(2)}) %collective-permute-start.3) | collective-permute-done | bytes 81952 | tf_op jit(solution)/shard_map/ppermute | solution.py:262
  18.5 0.0 copy-done.3
  18.5 0.0 copy-start
  18.5 0.0 copy-start.2
  18.5 2.1 %far_sums.1 = (f32[128,1024]{1,0:T(8,128)S(1)}, f32[128,1024]{1,0:T(8,128)S(1)}, f32[40,128]{1,0:T(8,128)S(1)}, f32[32,128]{1,0:T(8,128)S(1)}) custom-call(s32[3]{0:T(128)S(1)} %pad_add_fusion.place_ref, bf16[320,128]{1,0:T(8,128)(2,1)S(1)} %collective-permute-done.2.top_ref, bf16[320,128]{1,0:T(8,128)(2,1)S(1)} %collective-permute-done.3.bottom_ref, ...), custom_call_target="tpu_custom_call" | custom-call | flops 2000000000 | bytes 3000000 | tf_op jit(solution)/shard_map/far_sums/pallas_call | solution.py:244
  20.6 0.1 collective-permute-start.4
  20.7 1.6 %collective-permute-start.5 = (f32[40,128]{1,0:T(8,128)S(1)}, f32[40,128]{1,0:T(8,128)S(1)}, u32[]{:S(2)}, u32[]{:S(2)}) collective-permute-start(f32[40,128]{1,0:T(8,128)S(1)} %get-tuple-element.19), channel_id=1, source_target_pairs={{0,8},{1,9},{2,10},{3,11},{4,12},{5,13},{6,14},{7,15},{8,16},{9,17... | collective-permute-start | bytes 61448 | tf_op jit(solution)/shard_map/ppermute | solution.py:311
  22.3 1.3 %collective-permute-start.6 = (f32[32,128]{1,0:T(8,128)S(1)}, f32[32,128]{1,0:T(8,128)S(1)}, u32[]{:S(2)}, u32[]{:S(2)}) collective-permute-start(f32[32,128]{1,0:T(8,128)S(1)} %get-tuple-element.20), channel_id=1, source_target_pairs={{0,9},{1,8},{2,11},{3,10},{4,13},{5,12},{6,15},{7,14},{8,17},{9,16... | collective-permute-start | bytes 49160 | tf_op jit(solution)/shard_map/ppermute | solution.py:312
  23.6 0.0 collective-permute-done.4.got_ref
  23.6 0.3 code.1
  23.8 6.8 %collective-permute-done.6.cross_ref = f32[32,128]{1,0:T(8,128)S(1)} collective-permute-done((f32[32,128]{1,0:T(8,128)S(1)}, f32[32,128]{1,0:T(8,128)S(1)}, u32[]{:S(2)}, u32[]{:S(2)}) %collective-permute-start.6) | collective-permute-done | bytes 16416 | tf_op jit(solution)/shard_map/ppermute | solution.py:312
  30.6 0.1 collective-permute-done.5.over_ref
  30.7 21.2 %all_to_all.5.got_ref = s16[32,40,128]{2,1,0:T(8,128)(2,1)S(1)} all-to-all(s16[32,40,128]{2,1,0:T(8,128)(2,1)S(1)} %code.1), channel_id=1, replica_groups=mesh['node'=32,'local'=8] {'node'}, dimensions={0} | all-to-all | bytes 655360 | tf_op jit(solution)/shard_map/all_to_all | solution.py:314
  51.9 0.0 copy-done
  51.9 0.0 copy-done.2
  51.9 5.2 %update.1 = (f32[4096,128]{1,0:T(8,128)}, f32[32,128]{1,0:T(8,128)}) custom-call(s32[3]{0:T(128)S(1)} %pad_add_fusion.place_ref, s16[32,40,128]{2,1,0:T(8,128)(2,1)S(1)} %all_to_all.5.got_ref, f32[40,128]{1,0:T(8,128)S(1)} %collective-permute-done.5.over_ref, f32[32,128]{1,0:T(8,128)S(1)} %collective-permute-done.6.cross_ref, f32[4096,128]{1,0:T(8,128)S(1)} %copy-done, ...), custom_call_target="tpu_custom_call" | custom-call | tf_op jit(solution)/shard_map/update/pallas_call | solution.py:284
  (2 shorter events, 0.0 us)
Async XLA Ops:
  2.5 7.4 %collective-permute-start.1 = (bf16[640,128]{1,0:T(8,128)(2,1)}, bf16[640,128]{1,0:T(8,128)(2,1)S(1)}, u32[]{:S(2)}, u32[]{:S(2)}) collective-permute-start(bf16[640,128]{1,0:T(8,128)(2,1)} %prep.1.mine_ref), channel_id=1, source_target_pairs={{0,6},{1,7},{2,0},{3,1},{4,2},{5,3},{6,4},{7,5},{8,14},{9,15},{10,... | collective-permute-start | bytes 491528 | tf_op jit(solution)/shard_map/ppermute | solution.py:262
  3.2 6.6 %collective-permute-start = (bf16[640,128]{1,0:T(8,128)(2,1)}, bf16[640,128]{1,0:T(8,128)(2,1)S(1)}, u32[]{:S(2)}, u32[]{:S(2)}) collective-permute-start(bf16[640,128]{1,0:T(8,128)(2,1)} %prep.1.mine_ref), channel_id=1, source_target_pairs={{0,2},{1,3},{2,4},{3,5},{4,6},{5,7},{6,0},{7,1},{8,10},{9,11},{10,... | collective-permute-start | bytes 491528 | tf_op jit(solution)/shard_map/ppermute | solution.py:262
  5.8 0.9 %copy-start.1 = (bf16[640,128]{1,0:T(8,128)(2,1)S(1)}, bf16[640,128]{1,0:T(8,128)(2,1)}, u32[]{:S(2)}) copy-start(bf16[640,128]{1,0:T(8,128)(2,1)} %prep.1.mine_ref) | copy-start | bytes 491524
  9.8 8.7 %copy-start.3 = (s32[2048]{0:T(1024)S(1)}, s32[2048]{0:T(1024)}, u32[]{:S(2)}) copy-start(s32[2048]{0:T(1024)} %param.9) | copy-start | bytes 24580
  9.9 6.5 %collective-permute-start.2 = (bf16[320,128]{1,0:T(8,128)(2,1)S(1)}, bf16[320,128]{1,0:T(8,128)(2,1)S(1)}, u32[]{:S(2)}, u32[]{:S(2)}) collective-permute-start(bf16[320,128]{1,0:T(8,128)(2,1)S(1)} %slice.6), channel_id=1, source_target_pairs={{0,2},{1,3},{2,4},{3,5},{4,6},{5,7},{6,0},{7,1},{8,10},{9,11},{10,... | collective-permute-start | bytes 245768 | tf_op jit(solution)/shard_map/ppermute | solution.py:262
  12.9 5.7 %collective-permute-start.3 = (bf16[320,128]{1,0:T(8,128)(2,1)S(1)}, bf16[320,128]{1,0:T(8,128)(2,1)S(1)}, u32[]{:S(2)}, u32[]{:S(2)}) collective-permute-start(bf16[320,128]{1,0:T(8,128)(2,1)S(1)} %slice.7), channel_id=1, source_target_pairs={{0,6},{1,7},{2,0},{3,1},{4,2},{5,3},{6,4},{7,5},{8,14},{9,15},{10,... | collective-permute-start | bytes 245768 | tf_op jit(solution)/shard_map/ppermute | solution.py:262
  18.5 33.4 %copy-start = (f32[4096,128]{1,0:T(8,128)S(1)}, f32[4096,128]{1,0:T(8,128)}, u32[]{:S(2)}) copy-start(f32[4096,128]{1,0:T(8,128)} %table_ref.1) | copy-start | bytes 6291460
  18.5 33.4 %copy-start.2 = (f32[4096]{0:T(1024)S(1)}, f32[4096]{0:T(1024)}, u32[]{:S(2)}) copy-start(f32[4096]{0:T(1024)} %param.11) | copy-start | bytes 49156
  20.6 2.9 %collective-permute-start.4 = (f32[128,1024]{1,0:T(8,128)S(1)}, f32[128,1024]{1,0:T(8,128)S(1)}, u32[]{:S(2)}, u32[]{:S(2)}) collective-permute-start(f32[128,1024]{1,0:T(8,128)S(1)} %get-tuple-element.18), channel_id=1, source_target_pairs={{0,1},{1,0},{2,3},{3,2},{4,5},{5,4},{6,7},{7,6},{8,9},{9,8},{10,11... | collective-permute-start | bytes 1572872 | tf_op jit(solution)/shard_map/ppermute | solution.py:310
  20.7 10.0 %collective-permute-start.5 = (f32[40,128]{1,0:T(8,128)S(1)}, f32[40,128]{1,0:T(8,128)S(1)}, u32[]{:S(2)}, u32[]{:S(2)}) collective-permute-start(f32[40,128]{1,0:T(8,128)S(1)} %get-tuple-element.19), channel_id=1, source_target_pairs={{0,8},{1,9},{2,10},{3,11},{4,12},{5,13},{6,14},{7,15},{8,16},{9,17... | collective-permute-start | bytes 61448 | tf_op jit(solution)/shard_map/ppermute | solution.py:311
  22.3 8.3 %collective-permute-start.6 = (f32[32,128]{1,0:T(8,128)S(1)}, f32[32,128]{1,0:T(8,128)S(1)}, u32[]{:S(2)}, u32[]{:S(2)}) collective-permute-start(f32[32,128]{1,0:T(8,128)S(1)} %get-tuple-element.20), channel_id=1, source_target_pairs={{0,9},{1,8},{2,11},{3,10},{4,13},{5,12},{6,15},{7,14},{8,17},{9,16... | collective-permute-start | bytes 49160 | tf_op jit(solution)/shard_map/ppermute | solution.py:312

commit v4 on v3

--- a/solution.py
+++ b/solution.py
@@ -49,18 +49,17 @@
         out_ref[t * 128 : (t + 1) * 128, :] = perm_ref[t * 128 : (t + 1) * 128, :].T.astype(BF16)
 
 
-def add_sums(place_ref, pieces, low_ref, code_ref, counts_ref):
+def add_sums(place_ref, piece, low_ref, code_ref, counts_ref):
     chip, core = place_ref[0], place_ref[1]
     span = jnp.where(chip == 0, 2.0**34, jnp.where(chip == 1, 2.0**17, jnp.where(chip == 2, 1.0, 2.0**-17))).astype(F32)
-    for i, piece in enumerate(pieces):
-        mark = piece(512, 640).astype(F32) * span
-        valid = (mark >= 1.0) & (mark < 2.0**BLOCKS)
-        power = jnp.floor(jnp.log2(jnp.maximum(mark, 0.5)) + 0.002)
-        low_ref[i * 128 : (i + 1) * 128, :] = jnp.round((mark * jnp.exp2(-power) - 1.0) * 128.0)
-        block = jnp.clip(power, 0.0, 16.0).astype(I32)
-        block = jnp.where(block < 16, block ^ (core * 8), block)
-        member = (rows_iota(128, 128) >> 6) * 4 + (lanes_iota(128, 128) >> 5)
-        code_ref[i * 128 : (i + 1) * 128, :] = jnp.where(valid, block * GROUP + member, -1).astype(F32)
+    mark = piece(512, 640).astype(F32) * span
+    valid = (mark >= 1.0) & (mark < 2.0**BLOCKS)
+    power = jnp.floor(jnp.log2(jnp.maximum(mark, 0.5)) + 0.002)
+    low_ref[...] = jnp.round((mark * jnp.exp2(-power) - 1.0) * 128.0)
+    block = jnp.clip(power, 0.0, 16.0).astype(I32)
+    block = jnp.where(block < 16, block ^ (core * 8), block)
+    member = (rows_iota(128, 128) >> 6) * 4 + (lanes_iota(128, 128) >> 5)
+    code_ref[...] = jnp.where(valid, block * GROUP + member, -1).astype(F32)
 
     tiles = [(rows_iota(16, 128) + 16 * t).astype(F32).astype(BF16) for t in range(9)]
     one, zero = jnp.ones((16, 128), BF16), jnp.zeros((16, 128), BF16)
@@ -79,16 +78,15 @@
         )
 
     def step(i, carry):
-        row = (i // 32) * 128 + (i % 32) * 2
-        first, second = group_counts(row), group_counts(row + 1)
+        first, second = group_counts(i * 2), group_counts(i * 2 + 1)
         at = pl.multiple_of(i * 16, 16)
         for b in range(BLOCKS):
             both = jnp.concatenate([first[b * 8 : b * 8 + 8, :], second[b * 8 : b * 8 + 8, :]], axis=0)
             counts_ref[pl.ds(at, 16), b * 128 : (b + 1) * 128] = both.astype(BF16)
         return carry
 
-    lax.fori_loop(0, 32 * len(pieces), step, 0, unroll=32)
-    pooled = jnp.concatenate([piece(t * 128, t * 128 + 128) for piece in pieces for t in range(4)], axis=1)
+    lax.fori_loop(0, 32, step, 0, unroll=32)
+    pooled = jnp.concatenate([piece(t * 128, t * 128 + 128) for t in range(4)], axis=1)
     return jnp.dot(pooled, counts_ref[...], preferred_element_type=F32)
 
 
@@ -97,18 +95,15 @@
 
 
 def own_kernel(place_ref, mine_ref, total_ref, low_ref, code_ref, counts_ref):
-    total_ref[...] = add_sums(place_ref, [rows_of(mine_ref)], low_ref, code_ref, counts_ref)
-
-
-def near_kernel(place_ref, left_ref, right_ref, before_ref, total_ref, low_ref, code_ref, counts_ref):
-    pieces = [rows_of(left_ref), rows_of(right_ref)]
-    total_ref[...] = before_ref[...] + add_sums(place_ref, pieces, low_ref, code_ref, counts_ref)
-
-
-def far_kernel(place_ref, top_ref, bottom_ref, before_ref, row_ref, own_ref, other_ref, over_ref, cross_ref, low_ref, code_ref, counts_ref, far_ref):
-    far_ref[0:320, :] = top_ref[...]
-    far_ref[320:640, :] = bottom_ref[...]
-    total = before_ref[...] + add_sums(place_ref, [rows_of(far_ref)], low_ref, code_ref, counts_ref)
+    total_ref[...] = add_sums(place_ref, rows_of(mine_ref), low_ref, code_ref, counts_ref)
+
+
+def near_kernel(place_ref, near_ref, before_ref, total_ref, low_ref, code_ref, counts_ref):
+    total_ref[...] = before_ref[...] + add_sums(place_ref, rows_of(near_ref), low_ref, code_ref, counts_ref)
+
+
+def far_kernel(place_ref, far_ref, before_ref, row_ref, own_ref, other_ref, over_ref, cross_ref, low_ref, code_ref, counts_ref):
+    total = before_ref[...] + add_sums(place_ref, rows_of(far_ref), low_ref, code_ref, counts_ref)
     own_ref[...] = total[:, :1024]
     other_ref[...] = total[:, 1024:2048]
     over = total[:, 2048:].T
@@ -207,12 +202,13 @@
             accum = jnp.broadcast_to(accum_ref[line, :], (128, 128))
             fresh = jnp.sum(g * g * (1.0 / 128.0) + jnp.where(diag, accum, 0.0), axis=1, keepdims=True)
             accum_out[line, :] = jnp.sum(jnp.where(diag, fresh, 0.0), axis=0, keepdims=True)
-            step = LEARN_RATE * g / (jnp.sqrt(fresh) + EPSILON)
+            step = g * (LEARN_RATE / (jnp.sqrt(fresh) + EPSILON))
             at = slice(p * 256 + t * 128, p * 256 + t * 128 + 128)
             fresh_ref[at, :] = table_ref[at, :] - step
-        if p % 4 == 3:
-            done = pl.ds((p - 3) * 256, 1024)
-            copies.append(pltpu.make_async_copy(fresh_ref.at[done, :], table_out.at[done, :], sems.at[p // 4]))
+        if p in (9, 13, 15):
+            first = {9: 0, 13: 10, 15: 14}[p]
+            done = pl.ds(first * 256, (p + 1 - first) * 256)
+            copies.append(pltpu.make_async_copy(fresh_ref.at[done, :], table_out.at[done, :], sems.at[len(copies)]))
             copies[-1].start()
     for copy in copies:
         copy.wait()
@@ -240,33 +236,32 @@
     )(slot_t, lengths, pooled)
 
 
-def sums_call(kernel, name, pieces, outs, extra, *args):
+def sums_call(kernel, name, outs, *args):
     return pl.pallas_call(
         kernel,
         out_shape=[jax.ShapeDtypeStruct(shape, F32) for shape in outs],
         in_specs=[SMEM] + [VMEM] * (len(args) - 1),
         out_specs=[VMEM] * len(outs),
-        scratch_shapes=[
-            pltpu.VMEM((128 * pieces, 128), F32),
-            pltpu.VMEM((128 * pieces, 128), F32),
-            pltpu.VMEM((512 * pieces, BLOCKS * 128), BF16),
-        ]
-        + extra,
+        scratch_shapes=[pltpu.VMEM((128, 128), F32), pltpu.VMEM((128, 128), F32), pltpu.VMEM((512, WIDTH), BF16)],
         compiler_params=PARAMS,
-        cost_estimate=pl.CostEstimate(flops=2_000_000_000 * pieces, bytes_accessed=3_000_000, transcendentals=0),
+        cost_estimate=pl.CostEstimate(flops=2_000_000_000, bytes_accessed=3_000_000, transcendentals=0),
         name=name,
     )(*args)
 
 
 def gather_sums(place, packed, rows):
     shift = lambda x, k: lax.ppermute(x, "local", [(i, (i + k) % 8) for i in range(8)])
-    left, right = shift(packed, 2), shift(packed, 6)
-    (total,) = sums_call(own_kernel, "own_sums", 1, [(128, WIDTH)], [], place, packed)
-    left, right, total = lax.optimization_barrier((left, right, total))
-    top, bottom = shift(left[:320], 2), shift(right[320:], 6)
-    (total,) = sums_call(near_kernel, "near_sums", 2, [(128, WIDTH)], [], place, left, right, total)
+    right = shift(packed, 6)
+    (total,) = sums_call(own_kernel, "own_sums", [(128, WIDTH)], place, packed)
+    packed, total = lax.optimization_barrier((packed, total))
+    left = shift(packed, 2)
+    right, total = lax.optimization_barrier((right, total))
+    far = shift(right, 6)
+    (total,) = sums_call(near_kernel, "right_sums", [(128, WIDTH)], place, right, total)
+    left, total = lax.optimization_barrier((left, total))
+    (total,) = sums_call(near_kernel, "left_sums", [(128, WIDTH)], place, left, total)
     outs = [(128, 1024), (128, 1024), (40, 128), (32, 128)]
-    return sums_call(far_kernel, "far_sums", 1, outs, [pltpu.VMEM((640, 128), BF16)], place, top, bottom, total, rows)
+    return sums_call(far_kernel, "far_sums", outs, place, far, total, rows)
 
 
 def code(own, got, slot_row):
@@ -290,7 +285,7 @@
             pltpu.VMEM((1152, 256), BF16),
             pltpu.VMEM((24, 128), I32),
             pltpu.VMEM((4096, 128), F32),
-            pltpu.SemaphoreType.DMA((4,)),
+            pltpu.SemaphoreType.DMA((3,)),
         ],
         compiler_params=PARAMS,
         name="update",
@@ -310,8 +305,7 @@
     other = lax.ppermute(other, "local", [(i, i ^ 1) for i in range(8)])
     over = lax.ppermute(over, ("node", "local"), next_node(0))
     cross = lax.ppermute(cross, ("node", "local"), next_node(1))
-    codes, over, cross = lax.optimization_barrier((code(own, other, rows), over, cross))
-    codes = lax.all_to_all(codes, "node", split_axis=0, concat_axis=0, tiled=True)
+    codes = lax.all_to_all(code(own, other, rows), "node", split_axis=0, concat_axis=0, tiled=True)
     table_new, accum_new = update(place, codes, over, cross, table, accum.reshape(32, 128))
     return table_new, accum_new.reshape(4096)
 

time: 57.4 us -> 53 us (0.923)
  blocking collectives: 21.2 us -> 0 us
  waiting for transfers between devices: 10.2 us -> 18.4 us
  starting transfers between devices: 9.17 us -> 17 us
  Pallas kernels: 14.8 us -> 16.5 us
  local copies, waits for them, and re-layouts: 0.94 us -> 0.02 us
    all_to_all x1 -> x0, blocking collectives: 21.2 us -> none  [per_device(): lax.all_to_all(codes, 'node', split_axis=0, concat_axis=0, tiled=True)]
    all_to_all x0 -> x1, starting transfers between devices: none -> 11.3 us  [per_device(): lax.all_to_all(code(own, other, rows), 'node', split_axis=0, concat_axis=...]
    ppermute x4 -> x3, starting transfers between devices: 6.26 us -> 3.32 us  [gather_sums(): lax.ppermute(x, 'local', [(i, (i + k) % 8) for i in range(8)])]
    all_to_all x0 -> x1, waiting for transfers between devices: none -> 2.63 us  [per_device(): lax.all_to_all(code(own, other, rows), 'node', split_axis=0, concat_axis=...]
    ppermute x1, waiting for transfers between devices: 0.01 us -> 1.9 us  [per_device(): other = lax.ppermute(other, 'local', [(i, i ^ 1) for i in range(8)])]
    ppermute x1, waiting for transfers between devices: 0.1 us -> 1.68 us  [per_device(): over = lax.ppermute(over, ('node', 'local'), next_node(0))]
    ppermute x1, waiting for transfers between devices: 6.82 us -> 8.26 us  [per_device(): cross = lax.ppermute(cross, ('node', 'local'), next_node(1))]
    pallas_call x3 -> x4, Pallas kernels: 7.57 us -> 8.66 us  [sums_call(): pl.pallas_call(kernel, out_shape=[jax.ShapeDtypeStruct(shape, F32) for sh...]
  transfers between devices with their start and end apart: 7 -> 7, of which waited for: 4 -> 6; matrix products, arithmetic and copies ran while one was open for 0% -> 0% of each run, Pallas kernels for 10% -> 12%
where the time goes in v4:
time: 53 us; the launch traced here: 52.8 us
  waiting for transfers between devices  18.4 us (35%)
  starting transfers between devices  17 us (32%)
  Pallas kernels  16.5 us (31%)
  between operations  0.86 us (2%)
    all_to_all x1, starting transfers between devices, per_device(): lax.all_to_all(code(own, other, rows), 'node', split_axis=0, concat_axis=...  11.3 us
    pallas_call x4, Pallas kernels, sums_call(): pl.pallas_call(kernel, out_shape=[jax.ShapeDtypeStruct(shape, F32) for sh...  8.66 us
    ppermute x1, waiting for transfers between devices, per_device(): cross = lax.ppermute(cross, ('node', 'local'), next_node(1))  8.26 us
    pallas_call x1, Pallas kernels, update(): pl.pallas_call(update_kernel, out_shape=[jax.ShapeDtypeStruct((4096, 128)...  5.03 us
    ppermute x3, waiting for transfers between devices, gather_sums(): lax.ppermute(x, 'local', [(i, (i + k) % 8) for i in range(8)])  3.9 us
    ppermute x3, starting transfers between devices, gather_sums(): lax.ppermute(x, 'local', [(i, (i + k) % 8) for i in range(8)])  3.32 us
    all_to_all x1, waiting for transfers between devices, per_device(): lax.all_to_all(code(own, other, rows), 'node', split_axis=0, concat_axis=...  2.63 us
    ppermute x1, waiting for transfers between devices, per_device(): other = lax.ppermute(other, 'local', [(i, i ^ 1) for i in range(8)])  1.9 us
  transfers between devices with their start and end apart: 7, of which 6 were waited for; matrix products, arithmetic and copies ran while one was open for 0% of the time, Pallas kernels for 12%

profile of v4, /device:TPU:24, one launch (start us, length us, event | category | flops | bytes accessed | tf_op | source)
XLA Modules:
  0.0 52.8 jit_solution(10900758886640374664)
XLA Ops:
  0.6 1.8 %prep.1.mine_ref = bf16[640,128]{1,0:T(8,128)(2,1)} custom-call(s32[32,512]{1,0:T(8,128)} %bitcast.11, s32[1,512]{1,0:T(1,128)} %bitcast.12, bf16[512,128]{1,0:T(8,128)(2,1)} %pooled_ref.1), custom_call_target="tpu_custom_call" | custom-call | tf_op jit(solution)/shard_map/prep/pallas_call | solution.py:227
  2.5 0.7 %collective-permute-start = (bf16[640,128]{1,0:T(8,128)(2,1)}, bf16[640,128]{1,0:T(8,128)(2,1)S(1)}, u32[]{:S(2)}, u32[]{:S(2)}) collective-permute-start(bf16[640,128]{1,0:T(8,128)(2,1)} %prep.1.mine_ref), channel_id=1, source_target_pairs={{0,6},{1,7},{2,0},{3,1},{4,2},{5,3},{6,4},{7,5},{8,14},{9,15},{10,... | collective-permute-start | bytes 491528 | tf_op jit(solution)/shard_map/ppermute | solution.py:253
  3.2 0.1 pad_add_fusion.place_ref
  3.3 2.4 %own_sums.1.before_ref = f32[128,2176]{1,0:T(8,128)S(1)} custom-call(s32[3]{0:T(128)S(1)} %pad_add_fusion.place_ref, bf16[640,128]{1,0:T(8,128)(2,1)} %prep.1.mine_ref), custom_call_target="tpu_custom_call" | custom-call | flops 2000000000 | bytes 3000000 | tf_op jit(solution)/shard_map/own_sums/pallas_call | solution.py:240
  5.7 2.6 %collective-permute-start.2 = (bf16[640,128]{1,0:T(8,128)(2,1)}, bf16[640,128]{1,0:T(8,128)(2,1)S(1)}, u32[]{:S(2)}, u32[]{:S(2)}) collective-permute-start(bf16[640,128]{1,0:T(8,128)(2,1)} %prep.1.mine_ref), channel_id=1, source_target_pairs={{0,2},{1,3},{2,4},{3,5},{4,6},{5,7},{6,0},{7,1},{8,10},{9,11},{10,... | collective-permute-start | bytes 491528 | tf_op jit(solution)/shard_map/ppermute | solution.py:253
  8.3 1.5 %collective-permute-done.near_ref = bf16[640,128]{1,0:T(8,128)(2,1)S(1)} collective-permute-done((bf16[640,128]{1,0:T(8,128)(2,1)}, bf16[640,128]{1,0:T(8,128)(2,1)S(1)}, u32[]{:S(2)}, u32[]{:S(2)}) %collective-permute-start) | collective-permute-done | bytes 163872 | tf_op jit(solution)/shard_map/ppermute | solution.py:253
  9.8 0.0 collective-permute-start.1
  9.8 2.1 %right_sums.1.before_ref = f32[128,2176]{1,0:T(8,128)S(1)} custom-call(s32[3]{0:T(128)S(1)} %pad_add_fusion.place_ref, bf16[640,128]{1,0:T(8,128)(2,1)S(1)} %collective-permute-done.near_ref, f32[128,2176]{1,0:T(8,128)S(1)} %own_sums.1.before_ref), custom_call_target="tpu_custom_call" | custom-call | flops 2000000000 | bytes 3000000 | tf_op jit(solution)/shard_map/right_sums/pallas_call | solution.py:240
  11.9 0.0 copy-start.2
  11.9 0.0 collective-permute-done.2.near_ref
  11.9 2.1 %left_sums.1.before_ref = f32[128,2176]{1,0:T(8,128)S(1)} custom-call(s32[3]{0:T(128)S(1)} %pad_add_fusion.place_ref, bf16[640,128]{1,0:T(8,128)(2,1)S(1)} %collective-permute-done.2.near_ref, f32[128,2176]{1,0:T(8,128)S(1)} %right_sums.1.before_ref), custom_call_target="tpu_custom_call" | custom-call | flops 2000000000 | bytes 3000000 | tf_op jit(solution)/shard_map/left_sums/pallas_call | solution.py:240
  14.0 2.4 %collective-permute-done.1.far_ref = bf16[640,128]{1,0:T(8,128)(2,1)S(1)} collective-permute-done((bf16[640,128]{1,0:T(8,128)(2,1)S(1)}, bf16[640,128]{1,0:T(8,128)(2,1)S(1)}, u32[]{:S(2)}, u32[]{:S(2)}) %collective-permute-start.1) | collective-permute-done | bytes 163872 | tf_op jit(solution)/shard_map/ppermute | solution.py:253
  16.3 0.0 copy-done.2
  16.3 0.0 copy-start
  16.4 2.1 %far_sums.1 = (f32[128,1024]{1,0:T(8,128)S(1)}, f32[128,1024]{1,0:T(8,128)S(1)}, f32[40,128]{1,0:T(8,128)S(1)}, f32[32,128]{1,0:T(8,128)S(1)}) custom-call(s32[3]{0:T(128)S(1)} %pad_add_fusion.place_ref, bf16[640,128]{1,0:T(8,128)(2,1)S(1)} %collective-permute-done.1.far_ref, f32[128,2176]{1,0:T(8,128)S(1)} %left_sums.1.before_ref, s32[16,128]{1,0:T(8,128)S(1)} %bitcast.9), custom_call_target="tpu_custom_call" | custom-call | flops 2000000000 | bytes 3000000 | tf_op jit(solution)/shard_map/far_sums/pallas_call | solution.py:240
  18.5 0.0 copy-start.1
  18.5 0.1 collective-permute-start.3
  18.6 1.9 %collective-permute-done.3.got_ref = f32[128,1024]{1,0:T(8,128)S(1)} collective-permute-done((f32[128,1024]{1,0:T(8,128)S(1)}, f32[128,1024]{1,0:T(8,128)S(1)}, u32[]{:S(2)}, u32[]{:S(2)}) %collective-permute-start.3) | collective-permute-done | bytes 524320 | tf_op jit(solution)/shard_map/ppermute | solution.py:305
  20.5 1.0 %code.1 = s16[32,40,128]{2,1,0:T(8,128)(2,1)} custom-call(f32[128,1024]{1,0:T(8,128)S(1)} %get-tuple-element.20.own_ref, f32[128,1024]{1,0:T(8,128)S(1)} %collective-permute-done.3.got_ref, s32[16,128]{1,0:T(8,128)S(1)} %bitcast.10), custom_call_target="tpu_custom_call" | custom-call | tf_op jit(solution)/shard_map/code/pallas_call | solution.py:268
  21.5 11.3 %all-to-all-start = ((s16[32,40,128]{2,1,0:T(8,128)(2,1)}), s16[32,40,128]{2,1,0:T(8,128)(2,1)S(1)}, u32[]{:S(2)}, u32[]{:S(2)}) async-start(s16[32,40,128]{2,1,0:T(8,128)(2,1)} %code.1), calls=%async_computation | async-start | bytes 655360 | tf_op jit(solution)/shard_map/all_to_all | solution.py:308
  32.8 1.9 %collective-permute-start.4 = (f32[40,128]{1,0:T(8,128)S(1)}, f32[40,128]{1,0:T(8,128)S(1)}, u32[]{:S(2)}, u32[]{:S(2)}) collective-permute-start(f32[40,128]{1,0:T(8,128)S(1)} %get-tuple-element.22), channel_id=1, source_target_pairs={{0,8},{1,9},{2,10},{3,11},{4,12},{5,13},{6,14},{7,15},{8,16},{9,17... | collective-permute-start | bytes 61448 | tf_op jit(solution)/shard_map/ppermute | solution.py:306
  34.6 0.4 collective-permute-start.5
  35.0 8.3 %collective-permute-done.5.cross_ref = f32[32,128]{1,0:T(8,128)S(1)} collective-permute-done((f32[32,128]{1,0:T(8,128)S(1)}, f32[32,128]{1,0:T(8,128)S(1)}, u32[]{:S(2)}, u32[]{:S(2)}) %collective-permute-start.5) | collective-permute-done | bytes 16416 | tf_op jit(solution)/shard_map/ppermute | solution.py:307
  43.3 1.7 %collective-permute-done.4.over_ref = f32[40,128]{1,0:T(8,128)S(1)} collective-permute-done((f32[40,128]{1,0:T(8,128)S(1)}, f32[40,128]{1,0:T(8,128)S(1)}, u32[]{:S(2)}, u32[]{:S(2)}) %collective-permute-start.4) | collective-permute-done | bytes 20512 | tf_op jit(solution)/shard_map/ppermute | solution.py:306
  45.0 2.6 %all-to-all-done.got_ref = s16[32,40,128]{2,1,0:T(8,128)(2,1)S(1)} async-done(((s16[32,40,128]{2,1,0:T(8,128)(2,1)}), s16[32,40,128]{2,1,0:T(8,128)(2,1)S(1)}, u32[]{:S(2)}, u32[]{:S(2)}) %all-to-all-start) | async-done | bytes 327712 | tf_op jit(solution)/shard_map/all_to_all | solution.py:308
  47.6 0.0 copy-done
  47.6 0.0 copy-done.1
  47.6 5.0 %update.1 = (f32[4096,128]{1,0:T(8,128)}, f32[32,128]{1,0:T(8,128)}) custom-call(s32[3]{0:T(128)S(1)} %pad_add_fusion.place_ref, s16[32,40,128]{2,1,0:T(8,128)(2,1)S(1)} %all-to-all-done.got_ref, f32[40,128]{1,0:T(8,128)S(1)} %collective-permute-done.4.over_ref, f32[32,128]{1,0:T(8,128)S(1)} %collective-permute-done.5.cross_ref, f32[4096,128]{1,0:T(8,128)S(1)} %copy-done, ...), custom_call_target="tpu_custom_call" | custom-call | tf_op jit(solution)/shard_map/update/pallas_call | solution.py:279
Async XLA Ops:
  2.5 7.4 %collective-permute-start = (bf16[640,128]{1,0:T(8,128)(2,1)}, bf16[640,128]{1,0:T(8,128)(2,1)S(1)}, u32[]{:S(2)}, u32[]{:S(2)}) collective-permute-start(bf16[640,128]{1,0:T(8,128)(2,1)} %prep.1.mine_ref), channel_id=1, source_target_pairs={{0,6},{1,7},{2,0},{3,1},{4,2},{5,3},{6,4},{7,5},{8,14},{9,15},{10,... | collective-permute-start | bytes 491528 | tf_op jit(solution)/shard_map/ppermute | solution.py:253
  5.7 6.2 %collective-permute-start.2 = (bf16[640,128]{1,0:T(8,128)(2,1)}, bf16[640,128]{1,0:T(8,128)(2,1)S(1)}, u32[]{:S(2)}, u32[]{:S(2)}) collective-permute-start(bf16[640,128]{1,0:T(8,128)(2,1)} %prep.1.mine_ref), channel_id=1, source_target_pairs={{0,2},{1,3},{2,4},{3,5},{4,6},{5,7},{6,0},{7,1},{8,10},{9,11},{10,... | collective-permute-start | bytes 491528 | tf_op jit(solution)/shard_map/ppermute | solution.py:253
  9.8 6.5 %collective-permute-start.1 = (bf16[640,128]{1,0:T(8,128)(2,1)S(1)}, bf16[640,128]{1,0:T(8,128)(2,1)S(1)}, u32[]{:S(2)}, u32[]{:S(2)}) collective-permute-start(bf16[640,128]{1,0:T(8,128)(2,1)S(1)} %collective-permute-done.near_ref), channel_id=1, source_target_pairs={{0,6},{1,7},{2,0},{3,1},{4,2},{5,3},{6,4},{7,5},{8,14},{9,15},{10,... | collective-permute-start | bytes 491528 | tf_op jit(solution)/shard_map/ppermute | solution.py:253
  11.9 4.5 %copy-start.2 = (s32[2048]{0:T(1024)S(1)}, s32[2048]{0:T(1024)}, u32[]{:S(2)}) copy-start(s32[2048]{0:T(1024)} %param.9) | copy-start | bytes 24580
  16.3 31.2 %copy-start = (f32[4096,128]{1,0:T(8,128)S(1)}, f32[4096,128]{1,0:T(8,128)}, u32[]{:S(2)}) copy-start(f32[4096,128]{1,0:T(8,128)} %table_ref.1) | copy-start | bytes 6291460
  18.5 29.1 %copy-start.1 = (f32[4096]{0:T(1024)S(1)}, f32[4096]{0:T(1024)}, u32[]{:S(2)}) copy-start(f32[4096]{0:T(1024)} %param.11) | copy-start | bytes 49156
  18.5 2.0 %collective-permute-start.3 = (f32[128,1024]{1,0:T(8,128)S(1)}, f32[128,1024]{1,0:T(8,128)S(1)}, u32[]{:S(2)}, u32[]{:S(2)}) collective-permute-start(f32[128,1024]{1,0:T(8,128)S(1)} %get-tuple-element.21), channel_id=1, source_target_pairs={{0,1},{1,0},{2,3},{3,2},{4,5},{5,4},{6,7},{7,6},{8,9},{9,8},{10,11... | collective-permute-start | bytes 1572872 | tf_op jit(solution)/shard_map/ppermute | solution.py:305
  21.5 26.1 %all-to-all-start = ((s16[32,40,128]{2,1,0:T(8,128)(2,1)}), s16[32,40,128]{2,1,0:T(8,128)(2,1)S(1)}, u32[]{:S(2)}, u32[]{:S(2)}) async-start(s16[32,40,128]{2,1,0:T(8,128)(2,1)} %code.1), calls=%async_computation | async-start | bytes 655360 | tf_op jit(solution)/shard_map/all_to_all | solution.py:308
  32.8 12.2 %collective-permute-start.4 = (f32[40,128]{1,0:T(8,128)S(1)}, f32[40,128]{1,0:T(8,128)S(1)}, u32[]{:S(2)}, u32[]{:S(2)}) collective-permute-start(f32[40,128]{1,0:T(8,128)S(1)} %get-tuple-element.22), channel_id=1, source_target_pairs={{0,8},{1,9},{2,10},{3,11},{4,12},{5,13},{6,14},{7,15},{8,16},{9,17... | collective-permute-start | bytes 61448 | tf_op jit(solution)/shard_map/ppermute | solution.py:306
  34.6 8.6 %collective-permute-start.5 = (f32[32,128]{1,0:T(8,128)S(1)}, f32[32,128]{1,0:T(8,128)S(1)}, u32[]{:S(2)}, u32[]{:S(2)}) collective-permute-start(f32[32,128]{1,0:T(8,128)S(1)} %get-tuple-element.23), channel_id=1, source_target_pairs={{0,9},{1,8},{2,11},{3,10},{4,13},{5,12},{6,15},{7,14},{8,17},{9,16... | collective-permute-start | bytes 49160 | tf_op jit(solution)/shard_map/ppermute | solution.py:307

commit v5 on v4

--- a/solution.py
+++ b/solution.py
@@ -49,16 +49,16 @@
         out_ref[t * 128 : (t + 1) * 128, :] = perm_ref[t * 128 : (t + 1) * 128, :].T.astype(BF16)
 
 
-def add_sums(place_ref, piece, low_ref, code_ref, counts_ref):
+def add_sums(place_ref, pieces, low_ref, code_ref, counts_ref):
     chip, core = place_ref[0], place_ref[1]
     span = jnp.where(chip == 0, 2.0**34, jnp.where(chip == 1, 2.0**17, jnp.where(chip == 2, 1.0, 2.0**-17))).astype(F32)
-    mark = piece(512, 640).astype(F32) * span
+    mark = jnp.concatenate([piece(512, 640) for piece in pieces], axis=0).astype(F32) * span
     valid = (mark >= 1.0) & (mark < 2.0**BLOCKS)
     power = jnp.floor(jnp.log2(jnp.maximum(mark, 0.5)) + 0.002)
     low_ref[...] = jnp.round((mark * jnp.exp2(-power) - 1.0) * 128.0)
     block = jnp.clip(power, 0.0, 16.0).astype(I32)
     block = jnp.where(block < 16, block ^ (core * 8), block)
-    member = (rows_iota(128, 128) >> 6) * 4 + (lanes_iota(128, 128) >> 5)
+    member = ((rows_iota(*mark.shape) >> 6) & 1) * 4 + (lanes_iota(*mark.shape) >> 5)
     code_ref[...] = jnp.where(valid, block * GROUP + member, -1).astype(F32)
 
     tiles = [(rows_iota(16, 128) + 16 * t).astype(F32).astype(BF16) for t in range(9)]
@@ -78,15 +78,16 @@
         )
 
     def step(i, carry):
-        first, second = group_counts(i * 2), group_counts(i * 2 + 1)
+        row = (i // 32) * 128 + (i % 32) * 2
+        first, second = group_counts(row), group_counts(row + 1)
         at = pl.multiple_of(i * 16, 16)
         for b in range(BLOCKS):
             both = jnp.concatenate([first[b * 8 : b * 8 + 8, :], second[b * 8 : b * 8 + 8, :]], axis=0)
             counts_ref[pl.ds(at, 16), b * 128 : (b + 1) * 128] = both.astype(BF16)
         return carry
 
-    lax.fori_loop(0, 32, step, 0, unroll=32)
-    pooled = jnp.concatenate([piece(t * 128, t * 128 + 128) for t in range(4)], axis=1)
+    lax.fori_loop(0, 32 * len(pieces), step, 0, unroll=32)
+    pooled = jnp.concatenate([piece(t * 128, t * 128 + 128) for piece in pieces for t in range(4)], axis=1)
     return jnp.dot(pooled, counts_ref[...], preferred_element_type=F32)
 
 
@@ -95,15 +96,15 @@
 
 
 def own_kernel(place_ref, mine_ref, total_ref, low_ref, code_ref, counts_ref):
-    total_ref[...] = add_sums(place_ref, rows_of(mine_ref), low_ref, code_ref, counts_ref)
+    total_ref[...] = add_sums(place_ref, [rows_of(mine_ref)], low_ref, code_ref, counts_ref)
 
 
 def near_kernel(place_ref, near_ref, before_ref, total_ref, low_ref, code_ref, counts_ref):
-    total_ref[...] = before_ref[...] + add_sums(place_ref, rows_of(near_ref), low_ref, code_ref, counts_ref)
-
-
-def far_kernel(place_ref, far_ref, before_ref, row_ref, own_ref, other_ref, over_ref, cross_ref, low_ref, code_ref, counts_ref):
-    total = before_ref[...] + add_sums(place_ref, rows_of(far_ref), low_ref, code_ref, counts_ref)
+    total_ref[...] = before_ref[...] + add_sums(place_ref, [rows_of(near_ref)], low_ref, code_ref, counts_ref)
+
+
+def far_kernel(place_ref, right_ref, far_ref, before_ref, row_ref, own_ref, other_ref, over_ref, cross_ref, low_ref, code_ref, counts_ref):
+    total = before_ref[...] + add_sums(place_ref, [rows_of(right_ref), rows_of(far_ref)], low_ref, code_ref, counts_ref)
     own_ref[...] = total[:, :1024]
     other_ref[...] = total[:, 1024:2048]
     over = total[:, 2048:].T
@@ -236,32 +237,27 @@
     )(slot_t, lengths, pooled)
 
 
-def sums_call(kernel, name, outs, *args):
+def sums_call(kernel, name, pieces, outs, *args):
     return pl.pallas_call(
         kernel,
         out_shape=[jax.ShapeDtypeStruct(shape, F32) for shape in outs],
         in_specs=[SMEM] + [VMEM] * (len(args) - 1),
         out_specs=[VMEM] * len(outs),
-        scratch_shapes=[pltpu.VMEM((128, 128), F32), pltpu.VMEM((128, 128), F32), pltpu.VMEM((512, WIDTH), BF16)],
+        scratch_shapes=[pltpu.VMEM((128 * pieces, 128), F32), pltpu.VMEM((128 * pieces, 128), F32), pltpu.VMEM((512 * pieces, WIDTH), BF16)],
         compiler_params=PARAMS,
-        cost_estimate=pl.CostEstimate(flops=2_000_000_000, bytes_accessed=3_000_000, transcendentals=0),
+        cost_estimate=pl.CostEstimate(flops=2_000_000_000 * pieces, bytes_accessed=3_000_000, transcendentals=0),
         name=name,
     )(*args)
 
 
 def gather_sums(place, packed, rows):
     shift = lambda x, k: lax.ppermute(x, "local", [(i, (i + k) % 8) for i in range(8)])
-    right = shift(packed, 6)
-    (total,) = sums_call(own_kernel, "own_sums", [(128, WIDTH)], place, packed)
-    packed, total = lax.optimization_barrier((packed, total))
-    left = shift(packed, 2)
-    right, total = lax.optimization_barrier((right, total))
-    far = shift(right, 6)
-    (total,) = sums_call(near_kernel, "right_sums", [(128, WIDTH)], place, right, total)
+    left, right, far = shift(packed, 2), shift(packed, 6), shift(packed, 4)
+    (total,) = sums_call(own_kernel, "own_sums", 1, [(128, WIDTH)], place, packed)
     left, total = lax.optimization_barrier((left, total))
-    (total,) = sums_call(near_kernel, "left_sums", [(128, WIDTH)], place, left, total)
+    (total,) = sums_call(near_kernel, "left_sums", 1, [(128, WIDTH)], place, left, total)
     outs = [(128, 1024), (128, 1024), (40, 128), (32, 128)]
-    return sums_call(far_kernel, "far_sums", outs, place, far, total, rows)
+    return sums_call(far_kernel, "far_sums", 2, outs, place, right, far, total, rows)
 
 
 def code(own, got, slot_row):

time: 53 us -> 52.2 us (0.985)
  the two profiles are of different devices: /device:TPU:24 before, /device:TPU:16 now
where the time goes in v5:
time: 52.2 us; the launch traced here: 52 us
  starting transfers between devices  18.9 us (36%)
  waiting for transfers between devices  15.8 us (30%)
  Pallas kernels  15.4 us (30%)
  local copies, waits for them, and re-layouts  0.94 us (2%)
  between operations  0.88 us (2%)
    all_to_all x1, starting transfers between devices, per_device(): lax.all_to_all(code(own, other, rows), 'node', split_axis=0, concat_axis=...  11.3 us
    ppermute x1, waiting for transfers between devices, per_device(): cross = lax.ppermute(cross, ('node', 'local'), next_node(1))  8.26 us
    pallas_call x3, Pallas kernels, sums_call(): pl.pallas_call(kernel, out_shape=[jax.ShapeDtypeStruct(shape, F32) for sh...  7.6 us
    ppermute x3, starting transfers between devices, gather_sums(): lax.ppermute(x, 'local', [(i, (i + k) % 8) for i in range(8)])  5.31 us
    pallas_call x1, Pallas kernels, update(): pl.pallas_call(update_kernel, out_shape=[jax.ShapeDtypeStruct((4096, 128)...  5.04 us
    all_to_all x1, waiting for transfers between devices, per_device(): lax.all_to_all(code(own, other, rows), 'node', split_axis=0, concat_axis=...  2.63 us
    ppermute x1, waiting for transfers between devices, per_device(): other = lax.ppermute(other, 'local', [(i, i ^ 1) for i in range(8)])  1.9 us
    ppermute x1, starting transfers between devices, per_device(): over = lax.ppermute(over, ('node', 'local'), next_node(0))  1.87 us
  transfers between devices with their start and end apart: 7, of which 5 were waited for; matrix products, arithmetic and copies ran while one was open for 0% of the time, Pallas kernels for 8%

profile of v5, /device:TPU:16, one launch (start us, length us, event | category | flops | bytes accessed | tf_op | source)
XLA Modules:
  0.0 52.0 jit_solution(10050872123718860050)
XLA Ops:
  0.6 1.8 %prep.1.mine_ref = bf16[640,128]{1,0:T(8,128)(2,1)} custom-call(s32[32,512]{1,0:T(8,128)} %bitcast.11, s32[1,512]{1,0:T(1,128)} %bitcast.12, bf16[512,128]{1,0:T(8,128)(2,1)} %pooled_ref.1), custom_call_target="tpu_custom_call" | custom-call | tf_op jit(solution)/shard_map/prep/pallas_call | solution.py:228
  2.5 1.3 %collective-permute-start.2 = (bf16[640,128]{1,0:T(8,128)(2,1)}, bf16[640,128]{1,0:T(8,128)(2,1)S(1)}, u32[]{:S(2)}, u32[]{:S(2)}) collective-permute-start(bf16[640,128]{1,0:T(8,128)(2,1)} %prep.1.mine_ref), channel_id=1, source_target_pairs={{0,2},{1,3},{2,4},{3,5},{4,6},{5,7},{6,0},{7,1},{8,10},{9,11},{10,... | collective-permute-start | bytes 491528 | tf_op jit(solution)/shard_map/ppermute | solution.py:254
  3.7 0.7 %collective-permute-start = (bf16[640,128]{1,0:T(8,128)(2,1)}, bf16[640,128]{1,0:T(8,128)(2,1)S(1)}, u32[]{:S(2)}, u32[]{:S(2)}) collective-permute-start(bf16[640,128]{1,0:T(8,128)(2,1)} %prep.1.mine_ref), channel_id=1, source_target_pairs={{0,6},{1,7},{2,0},{3,1},{4,2},{5,3},{6,4},{7,5},{8,14},{9,15},{10,... | collective-permute-start | bytes 491528 | tf_op jit(solution)/shard_map/ppermute | solution.py:254
  4.5 3.3 %collective-permute-start.1 = (bf16[640,128]{1,0:T(8,128)(2,1)}, bf16[640,128]{1,0:T(8,128)(2,1)S(1)}, u32[]{:S(2)}, u32[]{:S(2)}) collective-permute-start(bf16[640,128]{1,0:T(8,128)(2,1)} %prep.1.mine_ref), channel_id=1, source_target_pairs={{0,4},{1,5},{2,6},{3,7},{4,0},{5,1},{6,2},{7,3},{8,12},{9,13},{10,... | collective-permute-start | bytes 491528 | tf_op jit(solution)/shard_map/ppermute | solution.py:254
  7.8 0.1 pad_add_fusion.place_ref
  7.8 0.0 copy-start.1
  7.8 0.9 %copy-done.1 = bf16[640,128]{1,0:T(8,128)(2,1)S(1)} copy-done((bf16[640,128]{1,0:T(8,128)(2,1)S(1)}, bf16[640,128]{1,0:T(8,128)(2,1)}, u32[]{:S(2)}) %copy-start.1) | copy-done | bytes 163864
  8.8 2.1 %own_sums.1.before_ref = f32[128,2176]{1,0:T(8,128)S(1)} custom-call(s32[3]{0:T(128)S(1)} %pad_add_fusion.place_ref, bf16[640,128]{1,0:T(8,128)(2,1)S(1)} %copy-done.1), custom_call_target="tpu_custom_call" | custom-call | flops 2000000000 | bytes 3000000 | tf_op jit(solution)/shard_map/own_sums/pallas_call | solution.py:241
  10.8 0.0 copy-start.3
  10.8 1.3 %collective-permute-done.2.near_ref = bf16[640,128]{1,0:T(8,128)(2,1)S(1)} collective-permute-done((bf16[640,128]{1,0:T(8,128)(2,1)}, bf16[640,128]{1,0:T(8,128)(2,1)S(1)}, u32[]{:S(2)}, u32[]{:S(2)}) %collective-permute-start.2) | collective-permute-done | bytes 163872 | tf_op jit(solution)/shard_map/ppermute | solution.py:254
  12.1 2.1 %left_sums.1.before_ref = f32[128,2176]{1,0:T(8,128)S(1)} custom-call(s32[3]{0:T(128)S(1)} %pad_add_fusion.place_ref, bf16[640,128]{1,0:T(8,128)(2,1)S(1)} %collective-permute-done.2.near_ref, f32[128,2176]{1,0:T(8,128)S(1)} %own_sums.1.before_ref), custom_call_target="tpu_custom_call" | custom-call | flops 2000000000 | bytes 3000000 | tf_op jit(solution)/shard_map/left_sums/pallas_call | solution.py:241
  14.2 0.0 collective-permute-done.right_ref
  14.2 0.0 collective-permute-done.1.far_ref
  14.2 0.0 copy-done.3
  14.2 0.0 copy-start
  14.2 0.0 copy-start.2
  14.2 3.5 %far_sums.1 = (f32[128,1024]{1,0:T(8,128)S(1)}, f32[128,1024]{1,0:T(8,128)S(1)}, f32[40,128]{1,0:T(8,128)S(1)}, f32[32,128]{1,0:T(8,128)S(1)}) custom-call(s32[3]{0:T(128)S(1)} %pad_add_fusion.place_ref, bf16[640,128]{1,0:T(8,128)(2,1)S(1)} %collective-permute-done.right_ref, bf16[640,128]{1,0:T(8,128)(2,1)S(1)} %collective-permute-done.1.far_ref, ...), custom_call_target="tpu_custom_call" | custom-call | flops 4000000000 | bytes 3000000 | tf_op jit(solution)/shard_map/far_sums/pallas_call | solution.py:241
  17.7 0.1 collective-permute-start.3
  17.8 1.9 %collective-permute-done.3.got_ref = f32[128,1024]{1,0:T(8,128)S(1)} collective-permute-done((f32[128,1024]{1,0:T(8,128)S(1)}, f32[128,1024]{1,0:T(8,128)S(1)}, u32[]{:S(2)}, u32[]{:S(2)}) %collective-permute-start.3) | collective-permute-done | bytes 524320 | tf_op jit(solution)/shard_map/ppermute | solution.py:301
  19.7 1.0 %code.1 = s16[32,40,128]{2,1,0:T(8,128)(2,1)} custom-call(f32[128,1024]{1,0:T(8,128)S(1)} %get-tuple-element.12.own_ref, f32[128,1024]{1,0:T(8,128)S(1)} %collective-permute-done.3.got_ref, s32[16,128]{1,0:T(8,128)S(1)} %bitcast.10), custom_call_target="tpu_custom_call" | custom-call | tf_op jit(solution)/shard_map/code/pallas_call | solution.py:264
  20.7 11.3 %all-to-all-start = ((s16[32,40,128]{2,1,0:T(8,128)(2,1)}), s16[32,40,128]{2,1,0:T(8,128)(2,1)S(1)}, u32[]{:S(2)}, u32[]{:S(2)}) async-start(s16[32,40,128]{2,1,0:T(8,128)(2,1)} %code.1), calls=%async_computation | async-start | bytes 655360 | tf_op jit(solution)/shard_map/all_to_all | solution.py:304
  32.0 1.9 %collective-permute-start.4 = (f32[40,128]{1,0:T(8,128)S(1)}, f32[40,128]{1,0:T(8,128)S(1)}, u32[]{:S(2)}, u32[]{:S(2)}) collective-permute-start(f32[40,128]{1,0:T(8,128)S(1)} %get-tuple-element.14), channel_id=1, source_target_pairs={{0,8},{1,9},{2,10},{3,11},{4,12},{5,13},{6,14},{7,15},{8,16},{9,17... | collective-permute-start | bytes 61448 | tf_op jit(solution)/shard_map/ppermute | solution.py:302
  33.9 0.4 collective-permute-start.5
  34.3 8.3 %collective-permute-done.5.cross_ref = f32[32,128]{1,0:T(8,128)S(1)} collective-permute-done((f32[32,128]{1,0:T(8,128)S(1)}, f32[32,128]{1,0:T(8,128)S(1)}, u32[]{:S(2)}, u32[]{:S(2)}) %collective-permute-start.5) | collective-permute-done | bytes 16416 | tf_op jit(solution)/shard_map/ppermute | solution.py:303
  42.5 1.7 %collective-permute-done.4.over_ref = f32[40,128]{1,0:T(8,128)S(1)} collective-permute-done((f32[40,128]{1,0:T(8,128)S(1)}, f32[40,128]{1,0:T(8,128)S(1)}, u32[]{:S(2)}, u32[]{:S(2)}) %collective-permute-start.4) | collective-permute-done | bytes 20512 | tf_op jit(solution)/shard_map/ppermute | solution.py:302
  44.2 2.6 %all-to-all-done.got_ref = s16[32,40,128]{2,1,0:T(8,128)(2,1)S(1)} async-done(((s16[32,40,128]{2,1,0:T(8,128)(2,1)}), s16[32,40,128]{2,1,0:T(8,128)(2,1)S(1)}, u32[]{:S(2)}, u32[]{:S(2)}) %all-to-all-start) | async-done | bytes 327712 | tf_op jit(solution)/shard_map/all_to_all | solution.py:304
  46.8 0.0 copy-done
  46.8 0.0 copy-done.2
  46.8 5.0 %update.1 = (f32[4096,128]{1,0:T(8,128)}, f32[32,128]{1,0:T(8,128)}) custom-call(s32[3]{0:T(128)S(1)} %pad_add_fusion.place_ref, s16[32,40,128]{2,1,0:T(8,128)(2,1)S(1)} %all-to-all-done.got_ref, f32[40,128]{1,0:T(8,128)S(1)} %collective-permute-done.4.over_ref, f32[32,128]{1,0:T(8,128)S(1)} %collective-permute-done.5.cross_ref, f32[4096,128]{1,0:T(8,128)S(1)} %copy-done, ...), custom_call_target="tpu_custom_call" | custom-call | tf_op jit(solution)/shard_map/update/pallas_call | solution.py:275
Async XLA Ops:
  2.5 9.7 %collective-permute-start.2 = (bf16[640,128]{1,0:T(8,128)(2,1)}, bf16[640,128]{1,0:T(8,128)(2,1)S(1)}, u32[]{:S(2)}, u32[]{:S(2)}) collective-permute-start(bf16[640,128]{1,0:T(8,128)(2,1)} %prep.1.mine_ref), channel_id=1, source_target_pairs={{0,2},{1,3},{2,4},{3,5},{4,6},{5,7},{6,0},{7,1},{8,10},{9,11},{10,... | collective-permute-start | bytes 491528 | tf_op jit(solution)/shard_map/ppermute | solution.py:254
  3.7 10.4 %collective-permute-start = (bf16[640,128]{1,0:T(8,128)(2,1)}, bf16[640,128]{1,0:T(8,128)(2,1)S(1)}, u32[]{:S(2)}, u32[]{:S(2)}) collective-permute-start(bf16[640,128]{1,0:T(8,128)(2,1)} %prep.1.mine_ref), channel_id=1, source_target_pairs={{0,6},{1,7},{2,0},{3,1},{4,2},{5,3},{6,4},{7,5},{8,14},{9,15},{10,... | collective-permute-start | bytes 491528 | tf_op jit(solution)/shard_map/ppermute | solution.py:254
  4.5 9.7 %collective-permute-start.1 = (bf16[640,128]{1,0:T(8,128)(2,1)}, bf16[640,128]{1,0:T(8,128)(2,1)S(1)}, u32[]{:S(2)}, u32[]{:S(2)}) collective-permute-start(bf16[640,128]{1,0:T(8,128)(2,1)} %prep.1.mine_ref), channel_id=1, source_target_pairs={{0,4},{1,5},{2,6},{3,7},{4,0},{5,1},{6,2},{7,3},{8,12},{9,13},{10,... | collective-permute-start | bytes 491528 | tf_op jit(solution)/shard_map/ppermute | solution.py:254
  7.8 0.9 %copy-start.1 = (bf16[640,128]{1,0:T(8,128)(2,1)S(1)}, bf16[640,128]{1,0:T(8,128)(2,1)}, u32[]{:S(2)}) copy-start(bf16[640,128]{1,0:T(8,128)(2,1)} %prep.1.mine_ref) | copy-start | bytes 491524
  10.8 3.4 %copy-start.3 = (s32[2048]{0:T(1024)S(1)}, s32[2048]{0:T(1024)}, u32[]{:S(2)}) copy-start(s32[2048]{0:T(1024)} %param.9) | copy-start | bytes 24580
  14.2 32.6 %copy-start = (f32[4096,128]{1,0:T(8,128)S(1)}, f32[4096,128]{1,0:T(8,128)}, u32[]{:S(2)}) copy-start(f32[4096,128]{1,0:T(8,128)} %table_ref.1) | copy-start | bytes 6291460
  14.2 32.6 %copy-start.2 = (f32[4096]{0:T(1024)S(1)}, f32[4096]{0:T(1024)}, u32[]{:S(2)}) copy-start(f32[4096]{0:T(1024)} %param.11) | copy-start | bytes 49156
  17.7 2.0 %collective-permute-start.3 = (f32[128,1024]{1,0:T(8,128)S(1)}, f32[128,1024]{1,0:T(8,128)S(1)}, u32[]{:S(2)}, u32[]{:S(2)}) collective-permute-start(f32[128,1024]{1,0:T(8,128)S(1)} %get-tuple-element.13), channel_id=1, source_target_pairs={{0,1},{1,0},{2,3},{3,2},{4,5},{5,4},{6,7},{7,6},{8,9},{9,8},{10,11... | collective-permute-start | bytes 1572872 | tf_op jit(solution)/shard_map/ppermute | solution.py:301
  20.7 26.1 %all-to-all-start = ((s16[32,40,128]{2,1,0:T(8,128)(2,1)}), s16[32,40,128]{2,1,0:T(8,128)(2,1)S(1)}, u32[]{:S(2)}, u32[]{:S(2)}) async-start(s16[32,40,128]{2,1,0:T(8,128)(2,1)} %code.1), calls=%async_computation | async-start | bytes 655360 | tf_op jit(solution)/shard_map/all_to_all | solution.py:304
  32.0 12.2 %collective-permute-start.4 = (f32[40,128]{1,0:T(8,128)S(1)}, f32[40,128]{1,0:T(8,128)S(1)}, u32[]{:S(2)}, u32[]{:S(2)}) collective-permute-start(f32[40,128]{1,0:T(8,128)S(1)} %get-tuple-element.14), channel_id=1, source_target_pairs={{0,8},{1,9},{2,10},{3,11},{4,12},{5,13},{6,14},{7,15},{8,16},{9,17... | collective-permute-start | bytes 61448 | tf_op jit(solution)/shard_map/ppermute | solution.py:302
  33.9 8.6 %collective-permute-start.5 = (f32[32,128]{1,0:T(8,128)S(1)}, f32[32,128]{1,0:T(8,128)S(1)}, u32[]{:S(2)}, u32[]{:S(2)}) collective-permute-start(f32[32,128]{1,0:T(8,128)S(1)} %get-tuple-element.15), channel_id=1, source_target_pairs={{0,9},{1,8},{2,11},{3,10},{4,13},{5,12},{6,15},{7,14},{8,17},{9,16... | collective-permute-start | bytes 49160 | tf_op jit(solution)/shard_map/ppermute | solution.py:303

commit v6 on v4

--- a/solution.py
+++ b/solution.py
@@ -251,15 +251,14 @@
 
 def gather_sums(place, packed, rows):
     shift = lambda x, k: lax.ppermute(x, "local", [(i, (i + k) % 8) for i in range(8)])
-    right = shift(packed, 6)
+    left, right = shift(packed, 2), shift(packed, 6)
     (total,) = sums_call(own_kernel, "own_sums", [(128, WIDTH)], place, packed)
     packed, total = lax.optimization_barrier((packed, total))
-    left = shift(packed, 2)
-    right, total = lax.optimization_barrier((right, total))
-    far = shift(right, 6)
-    (total,) = sums_call(near_kernel, "right_sums", [(128, WIDTH)], place, right, total)
+    far = shift(packed, 4)
     left, total = lax.optimization_barrier((left, total))
     (total,) = sums_call(near_kernel, "left_sums", [(128, WIDTH)], place, left, total)
+    right, total = lax.optimization_barrier((right, total))
+    (total,) = sums_call(near_kernel, "right_sums", [(128, WIDTH)], place, right, total)
     outs = [(128, 1024), (128, 1024), (40, 128), (32, 128)]
     return sums_call(far_kernel, "far_sums", outs, place, far, total, rows)
 

time: 53 us -> 50.9 us (0.960)
  starting transfers between devices: 17 us -> 14.5 us
    all_to_all x1, starting transfers between devices: 11.3 us -> 8.72 us  [per_device(): lax.all_to_all(code(own, other, rows), 'node', split_axis=0, concat_axis=...]
  transfers between devices with their start and end apart: 7 -> 7, of which waited for: 6 -> 6; matrix products, arithmetic and copies ran while one was open for 0% -> 0% of each run, Pallas kernels for 12% -> 13%
where the time goes in v6:
time: 50.9 us; the launch traced here: 50.6 us
  waiting for transfers between devices  18.6 us (37%)
  Pallas kernels  16.5 us (32%)
  starting transfers between devices  14.5 us (28%)
  between operations  0.87 us (2%)
    all_to_all x1, starting transfers between devices, per_device(): lax.all_to_all(code(own, other, rows), 'node', split_axis=0, concat_axis=...  8.72 us
    pallas_call x4, Pallas kernels, sums_call(): pl.pallas_call(kernel, out_shape=[jax.ShapeDtypeStruct(shape, F32) for sh...  8.66 us
    ppermute x1, waiting for transfers between devices, per_device(): cross = lax.ppermute(cross, ('node', 'local'), next_node(1))  8.26 us
    pallas_call x1, Pallas kernels, update(): pl.pallas_call(update_kernel, out_shape=[jax.ShapeDtypeStruct((4096, 128)...  5.04 us
    ppermute x3, waiting for transfers between devices, gather_sums(): lax.ppermute(x, 'local', [(i, (i + k) % 8) for i in range(8)])  4.1 us
    ppermute x3, starting transfers between devices, gather_sums(): lax.ppermute(x, 'local', [(i, (i + k) % 8) for i in range(8)])  3.51 us
    all_to_all x1, waiting for transfers between devices, per_device(): lax.all_to_all(code(own, other, rows), 'node', split_axis=0, concat_axis=...  2.63 us
    ppermute x1, waiting for transfers between devices, per_device(): other = lax.ppermute(other, 'local', [(i, i ^ 1) for i in range(8)])  1.9 us
  transfers between devices with their start and end apart: 7, of which 6 were waited for; matrix products, arithmetic and copies ran while one was open for 0% of the time, Pallas kernels for 13%

profile of v6, /device:TPU:24, one launch (start us, length us, event | category | flops | bytes accessed | tf_op | source)
XLA Modules:
  0.0 50.6 jit_solution(3628645962582530196)
XLA Ops:
  0.6 1.8 %prep.1.mine_ref = bf16[640,128]{1,0:T(8,128)(2,1)} custom-call(s32[32,512]{1,0:T(8,128)} %bitcast.11, s32[1,512]{1,0:T(1,128)} %bitcast.12, bf16[512,128]{1,0:T(8,128)(2,1)} %pooled_ref.1), custom_call_target="tpu_custom_call" | custom-call | tf_op jit(solution)/shard_map/prep/pallas_call | solution.py:227
  2.5 2.0 %collective-permute-start.2 = (bf16[640,128]{1,0:T(8,128)(2,1)}, bf16[640,128]{1,0:T(8,128)(2,1)S(1)}, u32[]{:S(2)}, u32[]{:S(2)}) collective-permute-start(bf16[640,128]{1,0:T(8,128)(2,1)} %prep.1.mine_ref), channel_id=1, source_target_pairs={{0,2},{1,3},{2,4},{3,5},{4,6},{5,7},{6,0},{7,1},{8,10},{9,11},{10,... | collective-permute-start | bytes 491528 | tf_op jit(solution)/shard_map/ppermute | solution.py:253
  4.4 0.1 collective-permute-start.1
  4.5 0.1 pad_add_fusion.place_ref
  4.6 2.4 %own_sums.1.before_ref = f32[128,2176]{1,0:T(8,128)S(1)} custom-call(s32[3]{0:T(128)S(1)} %pad_add_fusion.place_ref, bf16[640,128]{1,0:T(8,128)(2,1)} %prep.1.mine_ref), custom_call_target="tpu_custom_call" | custom-call | flops 2000000000 | bytes 3000000 | tf_op jit(solution)/shard_map/own_sums/pallas_call | solution.py:240
  7.0 1.5 %collective-permute-start = (bf16[640,128]{1,0:T(8,128)(2,1)}, bf16[640,128]{1,0:T(8,128)(2,1)S(1)}, u32[]{:S(2)}, u32[]{:S(2)}) collective-permute-start(bf16[640,128]{1,0:T(8,128)(2,1)} %prep.1.mine_ref), channel_id=1, source_target_pairs={{0,4},{1,5},{2,6},{3,7},{4,0},{5,1},{6,2},{7,3},{8,12},{9,13},{10,... | collective-permute-start | bytes 491528 | tf_op jit(solution)/shard_map/ppermute | solution.py:253
  8.5 0.1 collective-permute-done.2.near_ref
  8.6 2.1 %left_sums.1.before_ref = f32[128,2176]{1,0:T(8,128)S(1)} custom-call(s32[3]{0:T(128)S(1)} %pad_add_fusion.place_ref, bf16[640,128]{1,0:T(8,128)(2,1)S(1)} %collective-permute-done.2.near_ref, f32[128,2176]{1,0:T(8,128)S(1)} %own_sums.1.before_ref), custom_call_target="tpu_custom_call" | custom-call | flops 2000000000 | bytes 3000000 | tf_op jit(solution)/shard_map/left_sums/pallas_call | solution.py:240
  10.7 0.0 copy-start.2
  10.7 4.0 %collective-permute-done.1.near_ref = bf16[640,128]{1,0:T(8,128)(2,1)S(1)} collective-permute-done((bf16[640,128]{1,0:T(8,128)(2,1)}, bf16[640,128]{1,0:T(8,128)(2,1)S(1)}, u32[]{:S(2)}, u32[]{:S(2)}) %collective-permute-start.1) | collective-permute-done | bytes 163872 | tf_op jit(solution)/shard_map/ppermute | solution.py:253
  14.7 2.1 %right_sums.1.before_ref = f32[128,2176]{1,0:T(8,128)S(1)} custom-call(s32[3]{0:T(128)S(1)} %pad_add_fusion.place_ref, bf16[640,128]{1,0:T(8,128)(2,1)S(1)} %collective-permute-done.1.near_ref, f32[128,2176]{1,0:T(8,128)S(1)} %left_sums.1.before_ref), custom_call_target="tpu_custom_call" | custom-call | flops 2000000000 | bytes 3000000 | tf_op jit(solution)/shard_map/right_sums/pallas_call | solution.py:240
  16.7 0.0 collective-permute-done.far_ref
  16.7 0.0 copy-done.2
  16.8 0.0 copy-start
  16.8 2.1 %far_sums.1 = (f32[128,1024]{1,0:T(8,128)S(1)}, f32[128,1024]{1,0:T(8,128)S(1)}, f32[40,128]{1,0:T(8,128)S(1)}, f32[32,128]{1,0:T(8,128)S(1)}) custom-call(s32[3]{0:T(128)S(1)} %pad_add_fusion.place_ref, bf16[640,128]{1,0:T(8,128)(2,1)S(1)} %collective-permute-done.far_ref, f32[128,2176]{1,0:T(8,128)S(1)} %right_sums.1.before_ref, s32[16,128]{1,0:T(8,128)S(1)} %bitcast.9), custom_call_target="tpu_custom_call" | custom-call | flops 2000000000 | bytes 3000000 | tf_op jit(solution)/shard_map/far_sums/pallas_call | solution.py:240
  18.9 0.0 copy-start.1
  18.9 0.1 collective-permute-start.3
  19.0 1.9 %collective-permute-done.3.got_ref = f32[128,1024]{1,0:T(8,128)S(1)} collective-permute-done((f32[128,1024]{1,0:T(8,128)S(1)}, f32[128,1024]{1,0:T(8,128)S(1)}, u32[]{:S(2)}, u32[]{:S(2)}) %collective-permute-start.3) | collective-permute-done | bytes 524320 | tf_op jit(solution)/shard_map/ppermute | solution.py:304
  20.9 1.0 %code.1 = s16[32,40,128]{2,1,0:T(8,128)(2,1)} custom-call(f32[128,1024]{1,0:T(8,128)S(1)} %get-tuple-element.20.own_ref, f32[128,1024]{1,0:T(8,128)S(1)} %collective-permute-done.3.got_ref, s32[16,128]{1,0:T(8,128)S(1)} %bitcast.10), custom_call_target="tpu_custom_call" | custom-call | tf_op jit(solution)/shard_map/code/pallas_call | solution.py:267
  21.9 8.7 %all-to-all-start = ((s16[32,40,128]{2,1,0:T(8,128)(2,1)}), s16[32,40,128]{2,1,0:T(8,128)(2,1)S(1)}, u32[]{:S(2)}, u32[]{:S(2)}) async-start(s16[32,40,128]{2,1,0:T(8,128)(2,1)} %code.1), calls=%async_computation | async-start | bytes 655360 | tf_op jit(solution)/shard_map/all_to_all | solution.py:307
  30.6 1.9 %collective-permute-start.4 = (f32[40,128]{1,0:T(8,128)S(1)}, f32[40,128]{1,0:T(8,128)S(1)}, u32[]{:S(2)}, u32[]{:S(2)}) collective-permute-start(f32[40,128]{1,0:T(8,128)S(1)} %get-tuple-element.22), channel_id=1, source_target_pairs={{0,8},{1,9},{2,10},{3,11},{4,12},{5,13},{6,14},{7,15},{8,16},{9,17... | collective-permute-start | bytes 61448 | tf_op jit(solution)/shard_map/ppermute | solution.py:305
  32.5 0.4 collective-permute-start.5
  32.8 8.3 %collective-permute-done.5.cross_ref = f32[32,128]{1,0:T(8,128)S(1)} collective-permute-done((f32[32,128]{1,0:T(8,128)S(1)}, f32[32,128]{1,0:T(8,128)S(1)}, u32[]{:S(2)}, u32[]{:S(2)}) %collective-permute-start.5) | collective-permute-done | bytes 16416 | tf_op jit(solution)/shard_map/ppermute | solution.py:306
  41.1 1.7 %collective-permute-done.4.over_ref = f32[40,128]{1,0:T(8,128)S(1)} collective-permute-done((f32[40,128]{1,0:T(8,128)S(1)}, f32[40,128]{1,0:T(8,128)S(1)}, u32[]{:S(2)}, u32[]{:S(2)}) %collective-permute-start.4) | collective-permute-done | bytes 20512 | tf_op jit(solution)/shard_map/ppermute | solution.py:305
  42.8 2.6 %all-to-all-done.got_ref = s16[32,40,128]{2,1,0:T(8,128)(2,1)S(1)} async-done(((s16[32,40,128]{2,1,0:T(8,128)(2,1)}), s16[32,40,128]{2,1,0:T(8,128)(2,1)S(1)}, u32[]{:S(2)}, u32[]{:S(2)}) %all-to-all-start) | async-done | bytes 327712 | tf_op jit(solution)/shard_map/all_to_all | solution.py:307
  45.4 0.0 copy-done
  45.4 0.0 copy-done.1
  45.4 5.0 %update.1 = (f32[4096,128]{1,0:T(8,128)}, f32[32,128]{1,0:T(8,128)}) custom-call(s32[3]{0:T(128)S(1)} %pad_add_fusion.place_ref, s16[32,40,128]{2,1,0:T(8,128)(2,1)S(1)} %all-to-all-done.got_ref, f32[40,128]{1,0:T(8,128)S(1)} %collective-permute-done.4.over_ref, f32[32,128]{1,0:T(8,128)S(1)} %collective-permute-done.5.cross_ref, f32[4096,128]{1,0:T(8,128)S(1)} %copy-done, ...), custom_call_target="tpu_custom_call" | custom-call | tf_op jit(solution)/shard_map/update/pallas_call | solution.py:278
Async XLA Ops:
  2.5 6.2 %collective-permute-start.2 = (bf16[640,128]{1,0:T(8,128)(2,1)}, bf16[640,128]{1,0:T(8,128)(2,1)S(1)}, u32[]{:S(2)}, u32[]{:S(2)}) collective-permute-start(bf16[640,128]{1,0:T(8,128)(2,1)} %prep.1.mine_ref), channel_id=1, source_target_pairs={{0,2},{1,3},{2,4},{3,5},{4,6},{5,7},{6,0},{7,1},{8,10},{9,11},{10,... | collective-permute-start | bytes 491528 | tf_op jit(solution)/shard_map/ppermute | solution.py:253
  4.4 10.3 %collective-permute-start.1 = (bf16[640,128]{1,0:T(8,128)(2,1)}, bf16[640,128]{1,0:T(8,128)(2,1)S(1)}, u32[]{:S(2)}, u32[]{:S(2)}) collective-permute-start(bf16[640,128]{1,0:T(8,128)(2,1)} %prep.1.mine_ref), channel_id=1, source_target_pairs={{0,6},{1,7},{2,0},{3,1},{4,2},{5,3},{6,4},{7,5},{8,14},{9,15},{10,... | collective-permute-start | bytes 491528 | tf_op jit(solution)/shard_map/ppermute | solution.py:253
  7.0 9.7 %collective-permute-start = (bf16[640,128]{1,0:T(8,128)(2,1)}, bf16[640,128]{1,0:T(8,128)(2,1)S(1)}, u32[]{:S(2)}, u32[]{:S(2)}) collective-permute-start(bf16[640,128]{1,0:T(8,128)(2,1)} %prep.1.mine_ref), channel_id=1, source_target_pairs={{0,4},{1,5},{2,6},{3,7},{4,0},{5,1},{6,2},{7,3},{8,12},{9,13},{10,... | collective-permute-start | bytes 491528 | tf_op jit(solution)/shard_map/ppermute | solution.py:253
  10.7 6.1 %copy-start.2 = (s32[2048]{0:T(1024)S(1)}, s32[2048]{0:T(1024)}, u32[]{:S(2)}) copy-start(s32[2048]{0:T(1024)} %param.9) | copy-start | bytes 24580
  16.8 28.6 %copy-start = (f32[4096,128]{1,0:T(8,128)S(1)}, f32[4096,128]{1,0:T(8,128)}, u32[]{:S(2)}) copy-start(f32[4096,128]{1,0:T(8,128)} %table_ref.1) | copy-start | bytes 6291460
  18.9 26.5 %copy-start.1 = (f32[4096]{0:T(1024)S(1)}, f32[4096]{0:T(1024)}, u32[]{:S(2)}) copy-start(f32[4096]{0:T(1024)} %param.11) | copy-start | bytes 49156
  18.9 2.0 %collective-permute-start.3 = (f32[128,1024]{1,0:T(8,128)S(1)}, f32[128,1024]{1,0:T(8,128)S(1)}, u32[]{:S(2)}, u32[]{:S(2)}) collective-permute-start(f32[128,1024]{1,0:T(8,128)S(1)} %get-tuple-element.21), channel_id=1, source_target_pairs={{0,1},{1,0},{2,3},{3,2},{4,5},{5,4},{6,7},{7,6},{8,9},{9,8},{10,11... | collective-permute-start | bytes 1572872 | tf_op jit(solution)/shard_map/ppermute | solution.py:304
  21.9 23.5 %all-to-all-start = ((s16[32,40,128]{2,1,0:T(8,128)(2,1)}), s16[32,40,128]{2,1,0:T(8,128)(2,1)S(1)}, u32[]{:S(2)}, u32[]{:S(2)}) async-start(s16[32,40,128]{2,1,0:T(8,128)(2,1)} %code.1), calls=%async_computation | async-start | bytes 655360 | tf_op jit(solution)/shard_map/all_to_all | solution.py:307
  30.6 12.2 %collective-permute-start.4 = (f32[40,128]{1,0:T(8,128)S(1)}, f32[40,128]{1,0:T(8,128)S(1)}, u32[]{:S(2)}, u32[]{:S(2)}) collective-permute-start(f32[40,128]{1,0:T(8,128)S(1)} %get-tuple-element.22), channel_id=1, source_target_pairs={{0,8},{1,9},{2,10},{3,11},{4,12},{5,13},{6,14},{7,15},{8,16},{9,17... | collective-permute-start | bytes 61448 | tf_op jit(solution)/shard_map/ppermute | solution.py:305
  32.5 8.6 %collective-permute-start.5 = (f32[32,128]{1,0:T(8,128)S(1)}, f32[32,128]{1,0:T(8,128)S(1)}, u32[]{:S(2)}, u32[]{:S(2)}) collective-permute-start(f32[32,128]{1,0:T(8,128)S(1)} %get-tuple-element.23), channel_id=1, source_target_pairs={{0,9},{1,8},{2,11},{3,10},{4,13},{5,12},{6,15},{7,14},{8,17},{9,16... | collective-permute-start | bytes 49160 | tf_op jit(solution)/shard_map/ppermute | solution.py:306
